TPU v7x, 256 devices: a whole 4x4x8 slice. The times are simulated.
256 devices in a mesh: seq: 8 (over y, x_hi), dp: 32 (over z, x_lo, core).
Axes of the slice: x: 4 (x_hi: 2, x_lo: 2; x = x_hi * 2 + x_lo), y: 4, z: 8, core: 2. Of those that a mesh axis runs over, the one named last changes fastest.
Arguments:
- layer_input: bfloat16 [32, 2048, 8192], P('dp', 'seq'), may hold values from -400 to 400
- frozen_queries: bfloat16 [32, 2048, 6144], P('dp', 'seq'), may hold values from -70 to 70
- frozen_keys: bfloat16 [32, 2048, 768], P('dp', 'seq'), may hold values from -6 to 6
- frozen_values: bfloat16 [32, 2048, 768], P('dp', 'seq'), may hold values from -6 to 6
- output_gradient: bfloat16 [32, 2048, 6144], P('dp', 'seq'), may hold values from -6 to 6
- norm_scale_vector: bfloat16 [8192], replicated, may hold values from 0.5 to 1.5
- query_down_weight: bfloat16 [8, 8192], replicated, may hold values from -0.0625 to 0.0625
- query_up_weight: bfloat16 [8, 6144], replicated, may hold values from -2 to 2
- value_down_weight: bfloat16 [8, 8192], replicated, may hold values from -0.0625 to 0.0625
- value_up_weight: bfloat16 [8, 768], replicated, may hold values from -2 to 2
- head_ordering: int32 [6], replicated, may hold values from 0 to 5, each once
Outputs:
- grad_query_a: float32 [8, 8192], replicated
- grad_query_b: float32 [8, 6144], replicated
- grad_value_a: float32 [8, 8192], replicated
- grad_value_b: float32 [8, 768], replicated
- grad_gain: float32 [8192], replicated
Inputs may be any that keep to these rules, and one draw needn't show every extreme that they name: `head_ordering`: a permutation of the 6 key-value heads.
All inputs are finite; a program needn't handle non-finite values.
Results may differ from a plain program's by a relative error of at most 0.012.
The roundings to bfloat16 on the way count: a program that leaves them out, or rounds other values in their place, can miss the bound.
Values may be sent and summed in bfloat16 or wider, within the bound.
No kernel may reach another device: no remote copies, remote signals or barrier semaphores. Data moves between devices by JAX's collectives and lax.ppermute only.
A program may use at most 128 MiB of HBM per device.

v0:
```python
import math

import jax
import jax.numpy as jnp
from jax import lax
from jax.sharding import PartitionSpec as P

HEAD_SIZE = 128


EPS = 1e-05
ADAPTER_SCALE = 2.0


def from_behind(block, axis, distance):
    devices = range(lax.axis_size(axis))
    route = [((i - distance) % len(devices), i) for i in devices]
    return lax.ppermute(block, axis, route)


def attend(query_rows, key_rows, values, grad_out, allowed):
    factor = 1.0 / math.sqrt(query_rows.shape[-1])
    scores = (
        jnp.einsum("tgd,ud->gtu", query_rows, key_rows, preferred_element_type=jnp.float32) * factor
    )
    scores = jnp.where(allowed[None], scores, -jnp.inf)
    row_max = jnp.max(scores, axis=-1, keepdims=True)
    exponent = jnp.exp(scores - row_max)
    probs_full = exponent / jnp.sum(exponent, axis=-1, keepdims=True)
    weights = probs_full.astype(jnp.bfloat16)
    attended = jnp.einsum("gtu,ud->tgd", weights, values, preferred_element_type=jnp.float32)
    delta = jnp.sum(grad_out.astype(jnp.float32) * attended, axis=-1)
    dprob = jnp.einsum("tgd,ud->gtu", grad_out, values, preferred_element_type=jnp.float32)
    dscore = (probs_full * (dprob - delta.T[:, :, None])).astype(jnp.bfloat16)
    query_gradient = (
        jnp.einsum("gtu,ud->tgd", dscore, key_rows, preferred_element_type=jnp.float32) * factor
    )
    value_gradient = jnp.einsum(
        "gtu,tgd->ud", weights, grad_out, preferred_element_type=jnp.float32
    )
    return (query_gradient, value_gradient)


def attend_heads(operands):
    return attend(*operands)


def all_heads(query4, keys3, values3, grads4, allowed3):
    operands = (
        jnp.moveaxis(query4, 1, 0),
        jnp.moveaxis(keys3, 1, 0),
        jnp.moveaxis(values3, 1, 0),
        jnp.moveaxis(grads4, 1, 0),
        allowed3,
    )
    query_gradient, value_gradient = lax.map(attend_heads, operands)
    return (jnp.moveaxis(query_gradient, 0, 1), jnp.moveaxis(value_gradient, 0, 1))


def contracted_rows(left, right):
    return lax.dot_general(
        left, right, (((0,), (0,)), ((), ())), preferred_element_type=jnp.float32
    )


def contracted_columns(left, right):
    return lax.dot_general(
        left, right, (((1,), (1,)), ((), ())), preferred_element_type=jnp.float32
    )


def squares_of(parts):
    total = jnp.zeros((), jnp.float32)
    for part in parts:
        total = total + jnp.sum(part * part)
    return total


def shards(
    layer_input,
    frozen_queries,
    frozen_keys,
    frozen_values,
    output_gradient,
    norm_scale_vector,
    query_down_weight,
    query_up_weight,
    value_down_weight,
    value_up_weight,
    head_ordering,
):
    tok_rows = layer_input.shape[1]
    kv_heads = frozen_keys.shape[2] // HEAD_SIZE
    group_size = frozen_queries.shape[2] // frozen_keys.shape[2]
    hidden_f = layer_input[0].astype(jnp.float32)
    inverse = lax.rsqrt(jnp.mean(hidden_f * hidden_f, axis=-1, keepdims=True) + EPS)
    unit = hidden_f * inverse
    normalized_input = (unit * norm_scale_vector.astype(jnp.float32)).astype(jnp.bfloat16)
    query_inner = contracted_columns(normalized_input, query_down_weight).astype(jnp.bfloat16)
    value_inner = contracted_columns(normalized_input, value_down_weight).astype(jnp.bfloat16)
    query_rows = (
        frozen_queries[0].astype(jnp.float32)
        + ADAPTER_SCALE * jnp.dot(query_inner, query_up_weight, preferred_element_type=jnp.float32)
    ).astype(jnp.bfloat16)
    value_rows = (
        frozen_values[0].astype(jnp.float32)
        + ADAPTER_SCALE * jnp.dot(value_inner, value_up_weight, preferred_element_type=jnp.float32)
    ).astype(jnp.bfloat16)
    query4 = query_rows.reshape(tok_rows, kv_heads, group_size, HEAD_SIZE)
    keys3 = frozen_keys[0].reshape(tok_rows, kv_heads, HEAD_SIZE)
    values3 = value_rows.reshape(tok_rows, kv_heads, HEAD_SIZE)
    grads4 = output_gradient[0].reshape(tok_rows, kv_heads, group_size, HEAD_SIZE)
    head_ids = jnp.arange(kv_heads, dtype=jnp.int32)
    moved_ids = head_ordering[: kv_heads // 2]
    displaced_mask = jnp.any(moved_ids[:, None] == head_ids[None, :], axis=0)
    odd_place = lax.axis_index("seq") % 2 == 1
    needs_prior = jnp.logical_xor(displaced_mask, odd_place)
    prior = from_behind((keys3, values3), "seq", 1)
    prior_keys = prior[0]
    prior_values = prior[1]
    keys_ext = jnp.concatenate([prior_keys, keys3], axis=0)
    values_ext = jnp.concatenate([prior_values, values3], axis=0)
    query_pos = jnp.arange(tok_rows)[:, None]
    key_pos = jnp.arange(2 * tok_rows)[None, :]
    own_keys = (key_pos >= tok_rows) & (key_pos - tok_rows <= query_pos)
    prior_keys_mask = key_pos < tok_rows
    allowed3 = own_keys[None] | prior_keys_mask[None] & needs_prior[:, None, None]
    dq_full, dv_ext = all_heads(query4, keys_ext, values_ext, grads4, allowed3)
    handed = from_behind(dv_ext[:tok_rows].astype(jnp.bfloat16), "seq", -1).astype(jnp.float32)
    query_gradient = dq_full.astype(jnp.bfloat16)
    value_gradient = (dv_ext[tok_rows:] + handed).astype(jnp.bfloat16)
    query_gradient_rows = query_gradient.reshape(tok_rows, frozen_queries.shape[2])
    value_gradient_rows = value_gradient.reshape(tok_rows, frozen_keys.shape[2])
    query_up_unscaled = ADAPTER_SCALE * contracted_rows(query_inner, query_gradient_rows)
    value_up_unscaled = ADAPTER_SCALE * contracted_rows(value_inner, value_gradient_rows)
    query_gradient_inner = (
        ADAPTER_SCALE * contracted_columns(query_gradient_rows, query_up_weight)
    ).astype(jnp.bfloat16)
    value_gradient_inner = (
        ADAPTER_SCALE * contracted_columns(value_gradient_rows, value_up_weight)
    ).astype(jnp.bfloat16)
    raw_qa = contracted_rows(query_gradient_inner, normalized_input)
    raw_va = contracted_rows(value_gradient_inner, normalized_input)
    normalized_gradient = jnp.dot(
        query_gradient_inner, query_down_weight, preferred_element_type=jnp.float32
    ) + jnp.dot(value_gradient_inner, value_down_weight, preferred_element_type=jnp.float32)
    raw_gain = jnp.sum(normalized_gradient * unit, axis=0)
    listed_items = (
        query_down_weight.shape[0]
        * (
            query_down_weight.shape[1]
            + query_up_weight.shape[1]
            + value_down_weight.shape[1]
            + value_up_weight.shape[1]
        )
        + norm_scale_vector.shape[0]
    )
    limit = math.sqrt(listed_items)
    summed = lax.psum(
        (raw_qa, query_up_unscaled, raw_va, value_up_unscaled, raw_gain), ("seq", "dp")
    )
    factor = jnp.minimum(1.0, limit / jnp.sqrt(squares_of(summed)))
    return (
        summed[0] * factor,
        summed[1] * factor,
        summed[2] * factor,
        summed[3] * factor,
        summed[4] * factor,
    )


def solution(mesh):
    placed = (
        P("dp", "seq", None),
        P("dp", "seq", None),
        P("dp", "seq", None),
        P("dp", "seq", None),
        P("dp", "seq", None),
        P(),
        P(),
        P(),
        P(),
        P(),
        P(),
    )
    return jax.shard_map(
        shards, mesh=mesh, in_specs=placed, out_specs=(P(), P(), P(), P(), P()), check_vma=False
    )
```

profile of v0, /device:TPU:1, one launch (start us, length us, event | category | flops | bytes accessed | tf_op | source)
XLA Modules:
  0.0 431.5 jit_solution(16215854703528731421)
XLA Ops:
  7.2 1.9 copy.36
  9.2 3.6 collective-permute-start
  12.7 3.1 fusion.40
  17.1 1.9 copy-done.1
  23.4 3.4 convolution_convert_fusion.1
  27.4 3.1 fusion.44
  31.1 4.6 %copy.39 = bf16[1,256,6144]{1,2,0:T(8,128)(2,1)} copy(bf16[1,256,6144]{2,1,0:T(8,128)(2,1)} %param.17) | data formatting | bytes 6291456 | tf_op args[4]
  36.5 2.6 copy.65
  39.7 2.1 maximum_bitcast_fusion
  42.9 83.3 %while.12 = (s32[]{:T(128)}, bf16[6,256,8,128]{1,3,2,0:T(8,128)(2,1)}, f32[6,512,128]{1,2,0:T(8,128)}, bf16[6,512,128]{1,2,0:T(8,128)(2,1)}, pred[6,256,512]{1,2...) while((s32[]{:T(128)}, ...), condition=%wide.region_6.7_spmd, body=%wide.region_2.6_spmd.sunk | while | flops 1355807232 | bytes 50507916 | solution.py:56
  44.3 1.9 fusion.106
  46.2 1.8 fusion.107
  50.0 2.6 fusion.111
  52.6 4.3 fusion.110
  58.2 1.9 fusion.106
  60.1 1.8 fusion.107
  63.9 2.6 fusion.111
  66.5 4.3 fusion.110
  72.1 1.9 fusion.106
  74.0 1.8 fusion.107
  77.8 2.6 fusion.111
  80.4 4.2 fusion.110
  86.0 1.9 fusion.106
  87.8 1.8 fusion.107
  91.7 2.6 fusion.111
  94.2 4.2 fusion.110
  99.8 1.9 fusion.106
  101.7 1.8 fusion.107
  105.5 2.6 fusion.111
  108.1 4.2 fusion.110
  113.7 1.9 fusion.106
  115.6 1.8 fusion.107
  119.4 2.5 fusion.111
  121.9 4.3 fusion.110
  126.2 2.6 fusion.47
  128.8 3.6 convolution_multiply_fusion.1
  133.8 4.1 collective-permute-start.2
  137.9 4.5 %fusion.55 = f32[256,8192]{1,0:T(8,128)} fusion(bf16[256,8]{0,1:T(8,128)(2,1)S(1)} %fusion.47, bf16[8,8192]{1,0:T(8,128)(2,1)S(1)} %copy-done), kind=kOutput, calls=%fused_computation.94 | convolution fusion | flops 33554432 | bytes 8523776 | tf_op jit(solution)/shard_map/dot_general | solution.py:144
  142.4 2.6 collective-permute-done.2
  145.4 1.4 fusion.54
  146.8 6.4 %fusion.43 = f32[8192]{0:T(1024)S(1)} fusion(f32[256]{0:T(256)S(1)} %copy-done.15, bf16[1,256,8192]{2,1,0:T(8,128)(2,1)} %param.13, f32[256,8192]{1,0:T(8,128)} %fusion.55, bf16[256,8]{0,1:T(8,128)(2,1)S(1)} %fusion.48, bf16[8,8192]{1,0:T(8,128)(2,1)S(1)} %copy-done.6), kind=kOutput, calls=%fused_computation.53 | convolution fusion | flops 44032000 | bytes 12751872 | tf_op jit(solution)/shard_map/dot_general | solution.py:146
  153.5 81.9 %all-reduce = (f32[8,768]{1,0:T(8,128)S(1)}, f32[8192]{0:T(1024)S(1)}) all-reduce(f32[8,768]{1,0:T(8,128)S(1)} %convolution_multiply_fusion.3, f32[8192]{0:T(1024)S(1)} %fusion.43), channel_id=1, replica_groups=mesh['seq'=8,'dp'=32] {'seq','dp'}, use_global_device_ids=true, to_apply=%region_13.14 | all-reduce | flops 14336 | bytes 114688 | tf_op jit(solution)/shard_map/psum | solution.py:159
  236.6 175.2 %all-reduce.4.cloned.1.call-done = (f32[8,8192]{1,0:T(8,128)}, f32[8,6144]{1,0:T(8,128)}, f32[8,8192]{1,0:T(8,128)}) async-done(((f32[8,8192]{1,0:T(8,128)}, f32[8,6144]{1,0:T(8,128)}, f32[8,8192]{1,0:T(8,128)}), (f32[8,8192]{1,0:T(8,128)}, f32[8,6144]{1,0:T(8,128)}, f32[8,8192]{1,0:T(8,128)})) %all-reduce.4.cloned.1.call-update) | async-done | bytes 720912 | tf_op jit(solution)/shard_map/psum | solution.py:159
  411.9 1.6 multiply_reduce_fusion
  413.5 1.6 multiply_reduce_fusion.2
  415.1 1.6 multiply_reduce_fusion.1
  421.1 1.6 broadcast_multiply_fusion.2
  422.8 1.9 broadcast_multiply_fusion
  (107 shorter events, 33.7 us)
Async XLA Ops:
  7.2 16.2 %copy-start = (bf16[8,8192]{1,0:T(8,128)(2,1)S(1)}, bf16[8,8192]{1,0:T(8,128)(2,1)}, u32[]{:S(2)}) copy-start(bf16[8,8192]{1,0:T(8,128)(2,1)} %param.19) | copy-start | bytes 393220
  7.2 8.7 %copy-start.13 = (bf16[8192]{0:T(1024)(128)(2,1)S(1)}, bf16[8192]{0:T(1024)(128)(2,1)}, u32[]{:S(2)}) copy-start(bf16[8192]{0:T(1024)(128)(2,1)} %param.18) | copy-start | bytes 49156
  7.2 404.7 %all-reduce.4.cloned.1.call-start = ((), (), s32[]{:S(2)}) async-start(), calls=%async_computation | async-start | bytes 1441792 | tf_op jit(solution)/shard_map/psum | solution.py:159
  9.2 6.7 %copy-start.4 = (bf16[1,256,8192]{2,1,0:T(8,128)(2,1)S(1)}, bf16[1,256,8192]{2,1,0:T(8,128)(2,1)}, u32[]{:S(2)}) copy-start(bf16[1,256,8192]{2,1,0:T(8,128)(2,1)} %param.13) | copy-start | bytes 12582916
  9.2 30.5 %collective-permute-start = (bf16[256,6,128]{0,2,1:T(8,128)(2,1)}, bf16[256,6,128]{0,2,1:T(8,128)(2,1)}, u32[]{:S(2)}, u32[]{:S(2)}) collective-permute-start(bf16[256,6,128]{0,2,1:T(8,128)(2,1)} %bitcast.17), channel_id=1, source_target_pairs={{224,0},{0,32},{32,64},{64,96},{96,128},{128,160},{160,192},{192,2... | collective-permute-start | bytes 1179656 | tf_op jit(solution)/shard_map/ppermute | solution.py:18
  15.9 1.2 copy-start.14
  15.9 3.1 copy-start.6
  17.1 1.9 copy-start.1
  19.0 1.2 copy-start.8
  19.0 1.2 copy-start.9
  19.0 4.2 copy-start.17
  21.5 20.3 %collective-permute-start.1 = (bf16[256,6,128]{0,2,1:T(8,128)(2,1)}, bf16[256,6,128]{0,2,1:T(8,128)(2,1)}, u32[]{:S(2)}, u32[]{:S(2)}) collective-permute-start(bf16[256,6,128]{0,2,1:T(8,128)(2,1)} %bitcast.24), channel_id=1, source_target_pairs={{224,0},{0,32},{32,64},{64,96},{96,128},{128,160},{160,192},{192,2... | collective-permute-start | bytes 1179656 | tf_op jit(solution)/shard_map/ppermute | solution.py:18
  26.7 0.6 copy-start.10
  26.7 3.7 copy-start.16
  36.5 2.6 copy-start.12
  42.9 83.3 %copy-start.7 = (bf16[8,6144]{1,0:T(8,128)(2,1)S(1)}, bf16[8,6144]{1,0:T(8,128)(2,1)}, u32[]{:S(2)}) copy-start(bf16[8,6144]{1,0:T(8,128)(2,1)} %param.20) | copy-start | bytes 294916
  42.9 85.8 %copy-start.11 = (bf16[256,8]{0,1:T(8,128)(2,1)S(1)}, bf16[256,8]{0,1:T(8,128)(2,1)}, u32[]{:S(2)}) copy-start(bf16[256,8]{0,1:T(8,128)(2,1)} %copy-done.10) | copy-start | bytes 12292
  48.0 2.0 copy-start.3
  61.9 2.0 copy-start.3
  75.8 2.0 copy-start.3
  89.7 2.0 copy-start.3
  103.6 2.0 copy-start.3
  117.4 2.0 copy-start.3
  126.2 6.2 %copy-start.2 = (bf16[256,8192]{1,0:T(8,128)(2,1)S(1)}, bf16[256,8192]{1,0:T(8,128)(2,1)}, u32[]{:S(2)}) copy-start(bf16[256,8192]{1,0:T(8,128)(2,1)} %copy-done.1) | copy-start | bytes 12582916
  128.8 5.0 %copy-start.5 = (f32[6,512,128]{1,2,0:T(8,128)S(1)}, f32[6,512,128]{1,2,0:T(8,128)}, u32[]{:S(2)}) copy-start(f32[6,512,128]{1,2,0:T(8,128)} %get-tuple-element.49) | copy-start | bytes 4718596
  133.8 11.3 %collective-permute-start.2 = (bf16[256,6,128]{0,2,1:T(8,128)(2,1)S(1)}, bf16[256,6,128]{0,2,1:T(8,128)(2,1)S(1)}, u32[]{:S(2)}, u32[]{:S(2)}) collective-permute-start(bf16[256,6,128]{0,2,1:T(8,128)(2,1)S(1)} %slice.19), channel_id=1, source_target_pairs={{32,0},{64,32},{96,64},{128,96},{160,128},{192,160},{224,192},{0,2... | collective-permute-start | bytes 1179656 | tf_op jit(solution)/shard_map/ppermute | solution.py:18
  142.4 4.4 %copy-start.15 = (f32[256]{0:T(256)S(1)}, f32[256]{0:T(256)}, u32[]{:S(2)}) copy-start(f32[256]{0:T(256)} %copy-done.14) | copy-start | bytes 3076
Sparse Core Ops, SparseCore 0:
  153.4 258.4 all-reduce.3
where the time goes:
time: 434 us; the launch traced here: 431 us
  waiting for transfers between devices  178 us (41%)
  matrix products  86.9 us (20%)
  blocking collectives  81.9 us (19%)
  other arithmetic  33.8 us (8%)
  local copies, waits for them, and re-layouts  24.2 us (6%)
  between operations  17.5 us (4%)
  starting transfers between devices  8.98 us (2%)
    psum x1, waiting for transfers between devices, shards(): lax.psum((raw_qa, query_up_unscaled, raw_va, value_up_unscaled, raw_gain)...  175 us
    psum x1, blocking collectives, shards(): lax.psum((raw_qa, query_up_unscaled, raw_va, value_up_unscaled, raw_gain)...  81.9 us
    dot_general x6, matrix products, attend(): jnp.einsum('gtu,ud->tgd', dscore, key_rows, preferred_element_type=jnp.fl...  25.5 us
    dot_general x6, matrix products, attend(): jnp.einsum('gtu,tgd->ud', weights, grad_out, preferred_element_type=jnp.f...  15.4 us
    dot_general x6, matrix products, attend(): jnp.einsum('tgd,ud->gtu', query_rows, key_rows, preferred_element_type=jn...  11.1 us
    sub x6, other arithmetic, attend(): exponent = jnp.exp(scores - row_max)  11.1 us
    unnamed x37, local copies, waits for them, and re-layouts  9.64 us
    ppermute x3, starting transfers between devices, from_behind(): return lax.ppermute(block, axis, route)  8.94 us
  transfers between devices with their start and end apart: 4, of which 2 were waited for; matrix products, arithmetic and copies ran while one was open for 7% of the time, Pallas kernels for 0%

commit v1 on v0

v1 whole, which is shorter than its diff:
```python
import functools
import math

import jax
import jax.numpy as jnp
from jax import lax
from jax.experimental import pallas as pl
from jax.experimental.pallas import tpu as pltpu
from jax.sharding import PartitionSpec as P

HEAD_SIZE = 128
TOKENS = 256
HALF = 128
WIDTH = 8192
RANK = 8
KV_HEADS = 6
SHARE = 8
LANES = SHARE * HEAD_SIZE
EPS = 1e-05
FACTOR = 1.0 / math.sqrt(HEAD_SIZE)
LOG2_E = 1.4426950408889634
TILES = 96
QB_TILE = 64
F32 = jnp.float32
BF16 = jnp.bfloat16
BOTH = ("seq", "dp")
MIB = 1024 * 1024


def nn(left, right):
    return jnp.dot(left, right, preferred_element_type=F32)


def nt(left, right):
    return lax.dot_general(left, right, (((1,), (1,)), ((), ())), preferred_element_type=F32)


def norm_kernel(x_ref, scale_ref, down_ref, normed_ref, qm_ref, vm_ref, qmt_ref, vmt_ref):
    step = 1024
    total = jnp.zeros((HALF, HEAD_SIZE), F32)
    for start in range(0, WIDTH, HEAD_SIZE):
        part = x_ref[:, start : start + HEAD_SIZE].astype(F32)
        total = total + part * part
    mean = jnp.sum(total, axis=1, keepdims=True) * (1.0 / WIDTH)
    inverse = lax.rsqrt(mean + EPS)
    mid = jnp.zeros((HALF, 2 * RANK), F32)
    for start in range(0, WIDTH, step):
        cols = slice(start, start + step)
        unit = x_ref[:, cols].astype(F32) * inverse
        normed = (unit * scale_ref[:, cols].astype(F32)).astype(BF16)
        normed_ref[:, cols] = normed
        mid = mid + nt(normed, down_ref[:, cols])
    qm_ref[...] = mid[:, :RANK].astype(BF16)
    vm_ref[...] = mid[:, RANK:].astype(BF16)
    mid_t = mid.T
    qmt_ref[...] = mid_t[:RANK].astype(BF16)
    vmt_ref[...] = mid_t[RANK:].astype(BF16)


def attend_head(prior, q_ref, g_ref, k_ref, v_ref, qm, vm, qup, vup, kp, vp, q_scr, dq_scr):
    keys = k_ref[...]
    keys_t = keys.astype(F32).T.astype(BF16)
    values = (v_ref[...].astype(F32) + 2.0 * nn(vm, vup)).astype(BF16)
    q_scr[...] = (q_ref[...].astype(F32) + 2.0 * nn(qm, qup)).astype(BF16)
    key_id = lax.broadcasted_iota(jnp.int32, (HALF, 2 * HALF), 0)
    query_id = lax.broadcasted_iota(jnp.int32, (HALF, 2 * HALF), 1) % HALF
    allowed = key_id <= query_id
    if prior:
        kp_t = kp.astype(F32).T.astype(BF16)
    dv_low = dv_high = dv_prior = None
    for c in range(2):
        rows = slice(c * HALF, (c + 1) * HALF)
        near = (c + 1) * HALF
        for pair in range(SHARE // 2):
            cols = [slice(g * HEAD_SIZE, (g + 1) * HEAD_SIZE) for g in (2 * pair, 2 * pair + 1)]
            queries = jnp.concatenate([q_scr[rows, cols[0]], q_scr[rows, cols[1]]], axis=0)
            grads = jnp.concatenate([g_ref[rows, cols[0]], g_ref[rows, cols[1]]], axis=0)
            own = nt(keys[:near], queries) * (FACTOR * LOG2_E)
            diagonal = jnp.where(allowed, own[near - HALF :], -jnp.inf)
            parts = [diagonal] if c == 0 else [own[:HALF], diagonal]
            blocks = [(keys_t[:, j * HALF : (j + 1) * HALF], part) for j, part in enumerate(parts)]
            dprob = nt(values[:near], grads)
            dprobs = [dprob[j * HALF : (j + 1) * HALF] for j in range(c + 1)]
            if prior:
                parts.append(nt(kp, queries) * (FACTOR * LOG2_E))
                dprobs.append(nt(vp, grads))
            top = functools.reduce(jnp.maximum, [jnp.max(s, axis=0, keepdims=True) for s in parts])
            exps = [jnp.exp2(s - top) for s in parts]
            denom = functools.reduce(jnp.add, [jnp.sum(e, axis=0, keepdims=True) for e in exps])
            inv = 1.0 / denom
            probs = [e * inv for e in exps]
            weights = [p.astype(BF16) for p in probs]
            delta = functools.reduce(
                jnp.add,
                [jnp.sum(w.astype(F32) * d, axis=0, keepdims=True) for w, d in zip(weights, dprobs)],
            )
            dscore = [(p * (d - delta)).astype(BF16) for p, d in zip(probs, dprobs)]
            if c == 0:
                dq_t = nn(keys_t[:, :HALF], dscore[0])
                own_w = weights[0]
            else:
                dq_t = nn(keys_t, jnp.concatenate(dscore[:2], axis=0))
                own_w = jnp.concatenate(weights[:2], axis=0)
            if prior:
                dq_t = dq_t + nn(kp_t, dscore[-1])
                term = nn(weights[-1], grads)
                dv_prior = term if dv_prior is None else dv_prior + term
            dq_b = (dq_t * FACTOR).astype(BF16)
            dq_scr[cols[0], rows] = dq_b[:, :HALF]
            dq_scr[cols[1], rows] = dq_b[:, HALF:]
            term = nn(own_w, grads)
            dv_low = term[:HALF] if dv_low is None else dv_low + term[:HALF]
            if c == 1:
                dv_high = term[HALF:] if dv_high is None else dv_high + term[HALF:]
    dv = jnp.concatenate([dv_low, dv_high], axis=0).astype(BF16)
    return dv, dv_prior


def add_to(first, ref, value):
    @pl.when(first)
    def _():
        ref[...] = value

    @pl.when(jnp.logical_not(first))
    def _():
        ref[...] = ref[...] + value


def own_kernel(
    ids_ref, q_ref, g_ref, k_ref, v_ref, qm_ref, vm_ref, qmt_ref, vmt_ref, qup_ref, vup_ref,
    qb_ref, vb_ref, dqm_ref, dvm_ref, q_scr, dq_scr,
):
    first = pl.program_id(0) == 0
    qup, vup = qup_ref[...], vup_ref[...]
    dv, _ = attend_head(
        False, q_ref, g_ref, k_ref, v_ref, qm_ref[...], vm_ref[...], qup, vup, None, None, q_scr, dq_scr
    )
    dq_t = dq_scr[...]
    add_to(first, dqm_ref, 2.0 * nn(qup, dq_t))
    add_to(first, dvm_ref, 2.0 * nt(vup, dv))
    qb_ref[0] = 2.0 * nt(qmt_ref[...], dq_t)
    vb_ref[0] = 2.0 * nn(vmt_ref[...], dv)


def prior_kernel(
    ids_ref, q_ref, g_ref, k_ref, v_ref, qm_ref, vm_ref, qmt_ref, vmt_ref, qup_ref, vup_ref,
    kp_ref, vp_ref, vmtp_ref, qb_ref, vb_ref, dqm_ref, dvm_ref, dvp_ref, q_scr, dq_scr,
):
    first = pl.program_id(0) == 0
    qup, vup = qup_ref[...], vup_ref[...]
    vmt_prior = vmtp_ref[...]
    vm_prior = vmt_prior.astype(F32).T.astype(BF16)
    values_prior = (vp_ref[...].astype(F32) + 2.0 * nn(vm_prior, vup)).astype(BF16)
    dv, dv_prior = attend_head(
        True, q_ref, g_ref, k_ref, v_ref, qm_ref[...], vm_ref[...], qup, vup,
        kp_ref[...], values_prior, q_scr, dq_scr,
    )
    dv_prior = dv_prior.astype(BF16)
    dq_t = dq_scr[...]
    add_to(first, dqm_ref, 2.0 * nn(qup, dq_t))
    add_to(first, dvm_ref, 2.0 * nt(vup, dv))
    add_to(first, dvp_ref, 2.0 * nt(vup, dv_prior))
    qb_ref[0] = 2.0 * nt(qmt_ref[...], dq_t)
    vb_ref[0] = 2.0 * nn(vmt_ref[...], dv) + 2.0 * nn(vmt_prior, dv_prior)


def gather_kernel(
    ids_ref, normed_ref, dqm1_ref, dqm2_ref, dvm1_ref, dvm2_ref, dvh_ref,
    qb1_ref, vb1_ref, qb2_ref, vb2_ref, out_ref, buf,
):
    step = pl.program_id(0)

    @pl.when(step < 4)
    def _():
        dq = dqm1_ref[...] + dqm2_ref[...]
        dv = dvm1_ref[...] + dvm2_ref[...] + dvh_ref[...]
        mids = jnp.concatenate([dq, dv], axis=0).astype(BF16)
        for j in range(4):
            part = nn(mids, normed_ref[:, j * 512 : (j + 1) * 512]).astype(BF16)
            for k in range(4):
                out_ref[4 * j + k] = part[:, k * HEAD_SIZE : (k + 1) * HEAD_SIZE]

    @pl.when(step == 4)
    def _():
        buf[27:32] = jnp.zeros((5, 16, HEAD_SIZE), F32)
        for i in range(3):
            for base, qb_ref, vb_ref in ((0, qb2_ref, vb2_ref), (3, qb1_ref, vb1_ref)):
                head = ids_ref[base + i]
                upper = head >= 3
                row = pl.multiple_of(jnp.where(upper, 8, 0), 8)
                place = jnp.where(upper, head - 3, head)
                for k in range(SHARE):
                    buf[place * SHARE + k, pl.ds(row, 8), :] = qb_ref[i][:, k * HEAD_SIZE : (k + 1) * HEAD_SIZE]
                buf[24 + place, pl.ds(row, 8), :] = vb_ref[i]
        for t in range(16):
            out_ref[t] = buf[t].astype(BF16)

    @pl.when(step == 5)
    def _():
        for t in range(16):
            out_ref[t] = buf[16 + t].astype(BF16)


def clip_kernel(limit, sum_ref, qd_ref, vd_ref, scale_ref, qa_ref, qb_ref, va_ref, vb_ref, gain_ref, gains):
    total = jnp.zeros((16, HEAD_SIZE), F32)
    gain_total = jnp.zeros((1, HEAD_SIZE), F32)
    for t in range(QB_TILE):
        cols = slice(t * HEAD_SIZE, (t + 1) * HEAD_SIZE)
        tile = sum_ref[t].astype(F32)
        total = total + tile * tile
        mixed = qd_ref[:, cols].astype(F32) * tile[:RANK] + vd_ref[:, cols].astype(F32) * tile[RANK:]
        gain = jnp.sum(mixed, axis=0, keepdims=True) / scale_ref[:, cols].astype(F32)
        gains[:, cols] = gain
        gain_total = gain_total + gain * gain
    for t in range(QB_TILE, QB_TILE + 27):
        tile = sum_ref[t].astype(F32)
        total = total + tile * tile
    squares = jnp.sum(total, keepdims=True) + jnp.sum(gain_total, keepdims=True)
    factor = jnp.minimum(1.0, limit / jnp.sqrt(squares))
    gain_ref[...] = gains[...] * factor
    for t in range(QB_TILE):
        cols = slice(t * HEAD_SIZE, (t + 1) * HEAD_SIZE)
        tile = sum_ref[t].astype(F32) * factor
        qa_ref[:, cols] = tile[:RANK]
        va_ref[:, cols] = tile[RANK:]
    for t in range(24):
        tile = sum_ref[QB_TILE + t].astype(F32) * factor
        qb_ref[:, t * HEAD_SIZE : (t + 1) * HEAD_SIZE] = tile[:RANK]
        qb_ref[:, (24 + t) * HEAD_SIZE : (25 + t) * HEAD_SIZE] = tile[RANK:]
    for t in range(3):
        tile = sum_ref[QB_TILE + 24 + t].astype(F32) * factor
        vb_ref[:, t * HEAD_SIZE : (t + 1) * HEAD_SIZE] = tile[:RANK]
        vb_ref[:, (3 + t) * HEAD_SIZE : (4 + t) * HEAD_SIZE] = tile[RANK:]


def groups_along(keys):
    found = {}
    for device in range(256):
        y, xh, z, rest = device // 64, device // 32 % 2, device // 4 % 8, device % 4
        place = {"y": y, "xh": xh, "z": z, "xl": rest // 2, "core": rest % 2}
        found.setdefault(tuple(v for k, v in place.items() if k not in keys), []).append(device)
    return list(found.values())


PLANE = groups_along(("y", "xh", "xl", "core"))
COLUMN = groups_along(("z",))


def exchange(array, groups):
    return lax.all_to_all(array, BOTH, 0, 0, tiled=True, axis_index_groups=groups)


def sum_over_devices(tiles):
    shares = tiles.reshape(32, 3, 16, HEAD_SIZE)
    mine = jnp.sum(exchange(shares, PLANE).astype(F32), axis=0)
    copies = jnp.broadcast_to(mine[None], (8, 3, 16, HEAD_SIZE))
    mine = jnp.sum(exchange(copies, COLUMN), axis=0).astype(BF16)
    copies = jnp.broadcast_to(mine[None], (32, 3, 16, HEAD_SIZE))
    return exchange(copies, PLANE).reshape(TILES, 16, HEAD_SIZE)


def from_behind(block, distance):
    return lax.ppermute(block, "seq", [((i - distance) % 8, i) for i in range(8)])


def whole(shape):
    return pl.BlockSpec(shape, lambda *_: (0,) * len(shape))


def params(mib):
    return pltpu.CompilerParams(vmem_limit_bytes=mib * MIB)


def attention_call(prior, base, ids, q, g, k, v, qm, vm, qmt, vmt, qup, vup, extra):
    def by_head(rows, cols):
        return pl.BlockSpec((rows, cols), lambda i, ids: (0, ids[base + i]))

    in_specs = [
        by_head(TOKENS, LANES), by_head(TOKENS, LANES), by_head(TOKENS, HEAD_SIZE), by_head(TOKENS, HEAD_SIZE),
        whole((TOKENS, RANK)), whole((TOKENS, RANK)), whole((RANK, TOKENS)), whole((RANK, TOKENS)),
        by_head(RANK, LANES), by_head(RANK, HEAD_SIZE),
    ]
    if prior:
        in_specs += [by_head(TOKENS, HEAD_SIZE), by_head(TOKENS, HEAD_SIZE), whole((RANK, TOKENS))]
    mids = 3 if prior else 2
    return pl.pallas_call(
        prior_kernel if prior else own_kernel,
        out_shape=[
            jax.ShapeDtypeStruct((3, RANK, LANES), F32),
            jax.ShapeDtypeStruct((3, RANK, HEAD_SIZE), F32),
        ]
        + [jax.ShapeDtypeStruct((RANK, TOKENS), F32)] * mids,
        grid_spec=pltpu.PrefetchScalarGridSpec(
            num_scalar_prefetch=1,
            grid=(3,),
            in_specs=in_specs,
            out_specs=[
                pl.BlockSpec((1, RANK, LANES), lambda i, ids: (i, 0, 0)),
                pl.BlockSpec((1, RANK, HEAD_SIZE), lambda i, ids: (i, 0, 0)),
            ]
            + [whole((RANK, TOKENS))] * mids,
            scratch_shapes=[pltpu.VMEM((TOKENS, LANES), BF16), pltpu.VMEM((LANES, TOKENS), BF16)],
        ),
        compiler_params=params(24),
        cost_estimate=pl.CostEstimate(
            flops=(2 if prior else 1) * 3_000_000_000, bytes_accessed=4_000_000, transcendentals=0
        ),
        name="prior_attention" if prior else "own_attention",
    )(ids, q, g, k, v, qm, vm, qmt, vmt, qup, vup, *extra)


def shards(
    layer_input,
    frozen_queries,
    frozen_keys,
    frozen_values,
    output_gradient,
    norm_scale_vector,
    query_down_weight,
    query_up_weight,
    value_down_weight,
    value_up_weight,
    head_ordering,
):
    x, q, k, v, g = (
        a[0] for a in (layer_input, frozen_queries, frozen_keys, frozen_values, output_gradient)
    )
    keys_prior = from_behind(k, 1)
    values_prior = from_behind(v, 1)
    odd = lax.axis_index("seq") % 2 == 1
    ids = jnp.where(odd, jnp.roll(head_ordering, 3), head_ordering)
    down = jnp.concatenate([query_down_weight, value_down_weight], axis=0)
    scale = norm_scale_vector.reshape(1, WIDTH)

    normed, qm, vm, qmt, vmt = pl.pallas_call(
        norm_kernel,
        out_shape=[
            jax.ShapeDtypeStruct((TOKENS, WIDTH), BF16),
            jax.ShapeDtypeStruct((TOKENS, RANK), BF16),
            jax.ShapeDtypeStruct((TOKENS, RANK), BF16),
            jax.ShapeDtypeStruct((RANK, TOKENS), BF16),
            jax.ShapeDtypeStruct((RANK, TOKENS), BF16),
        ],
        grid=(2,),
        in_specs=[
            pl.BlockSpec((HALF, WIDTH), lambda i: (i, 0)),
            whole((1, WIDTH)),
            whole((2 * RANK, WIDTH)),
        ],
        out_specs=[
            pl.BlockSpec((HALF, WIDTH), lambda i: (i, 0)),
            pl.BlockSpec((HALF, RANK), lambda i: (i, 0)),
            pl.BlockSpec((HALF, RANK), lambda i: (i, 0)),
            pl.BlockSpec((RANK, HALF), lambda i: (0, i)),
            pl.BlockSpec((RANK, HALF), lambda i: (0, i)),
        ],
        compiler_params=params(24),
        name="norm",
    )(x, scale, down)

    vmt_prior = from_behind(vmt, 1)
    shared = (ids, q, g, k, v, qm, vm, qmt, vmt, query_up_weight, value_up_weight)
    qb1, vb1, dqm1, dvm1 = attention_call(False, 3, *shared, ())
    qb2, vb2, dqm2, dvm2, dvp = attention_call(
        True, 0, *shared, (keys_prior, values_prior, vmt_prior)
    )
    handed = from_behind(dvp, -1)

    tiles = pl.pallas_call(
        gather_kernel,
        out_shape=jax.ShapeDtypeStruct((TILES, 16, HEAD_SIZE), BF16),
        grid_spec=pltpu.PrefetchScalarGridSpec(
            num_scalar_prefetch=1,
            grid=(6,),
            in_specs=[pl.BlockSpec((TOKENS, 2048), lambda i, ids: (0, jnp.minimum(i, 3)))]
            + [whole((RANK, TOKENS))] * 5
            + [whole((3, RANK, LANES)), whole((3, RANK, HEAD_SIZE))] * 2,
            out_specs=pl.BlockSpec((16, 16, HEAD_SIZE), lambda i, ids: (i, 0, 0)),
            scratch_shapes=[pltpu.VMEM((32, 16, HEAD_SIZE), F32)],
        ),
        compiler_params=params(16),
        name="gradients",
    )(ids, normed, dqm1, dqm2, dvm1, dvm2, handed, qb1, vb1, qb2, vb2)

    summed = sum_over_devices(tiles)

    listed_items = RANK * (2 * WIDTH + KV_HEADS * LANES + KV_HEADS * HEAD_SIZE) + WIDTH
    qa, qb, va, vb, gain = pl.pallas_call(
        functools.partial(clip_kernel, math.sqrt(listed_items)),
        out_shape=[
            jax.ShapeDtypeStruct((RANK, WIDTH), F32),
            jax.ShapeDtypeStruct((RANK, KV_HEADS * LANES), F32),
            jax.ShapeDtypeStruct((RANK, WIDTH), F32),
            jax.ShapeDtypeStruct((RANK, KV_HEADS * HEAD_SIZE), F32),
            jax.ShapeDtypeStruct((1, WIDTH), F32),
        ],
        scratch_shapes=[pltpu.VMEM((1, WIDTH), F32)],
        compiler_params=params(16),
        name="clip",
    )(summed, query_down_weight, value_down_weight, scale)
    return (qa, qb, va, vb, gain.reshape(WIDTH))


def solution(mesh):
    placed = P("dp", "seq", None)
    return jax.shard_map(
        shards,
        mesh=mesh,
        in_specs=(placed,) * 5 + (P(),) * 6,
        out_specs=(P(), P(), P(), P(), P()),
        check_vma=False,
    )
```

time: 434 us -> 121 us (0.28)
  waiting for transfers between devices: 178 us -> 17.9 us
  matrix products: 86.9 us -> 0 us
  Pallas kernels: 0 us -> 35.4 us
  other arithmetic: 33.8 us -> 1.15 us
  blocking collectives: 81.9 us -> 50.8 us
  local copies, waits for them, and re-layouts: 24.2 us -> 6.96 us
  between operations: 17.5 us -> 0.79 us
    psum x1 -> x0, waiting for transfers between devices: 175 us -> none  [shards(): lax.psum((raw_qa, query_up_unscaled, raw_va, value_up_unscaled, raw_gain)...]
    dot_general x36 -> x0, matrix products: 86.9 us -> none  [the longest x6 25.5 us: attend(): jnp.einsum('gtu,ud->tgd', dscore, key_rows, preferred_element_type=jnp.fl...]
    psum x1 -> x0, blocking collectives: 81.9 us -> none  [shards(): lax.psum((raw_qa, query_up_unscaled, raw_va, value_up_unscaled, raw_gain)...]
    all_to_all x0 -> x3, blocking collectives: none -> 50.8 us  [exchange(): lax.all_to_all(array, BOTH, 0, 0, tiled=True, axis_index_groups=groups)]
    pallas_call x0 -> x5, Pallas kernels: none -> 35.4 us  [the longest x2 29.6 us: attention_call(): pl.pallas_call(prior_kernel if prior else own_kernel, out_shape=[jax.Shap...]
    ppermute x3 -> x4, waiting for transfers between devices: 2.65 us -> 17.9 us  [from_behind(): lax.ppermute(block, 'seq', [((i - distance) % 8, i) for i in range(8)])]
    sub x7 -> x0, other arithmetic: 11.1 us -> none  [the longest x6 11.1 us: attend(): exponent = jnp.exp(scores - row_max)]
    reduce_sum x6 -> x2, other arithmetic: 9.17 us -> 0.09 us  [the longest x1 0.07 us: sum_over_devices(): mine = jnp.sum(exchange(shares, PLANE).astype(F32), axis=0)]
  transfers between devices with their start and end apart: 4 -> 4, of which waited for: 2 -> 2; matrix products, arithmetic and copies ran while one was open for 7% -> 0% of each run, Pallas kernels for 0% -> 10%
where the time goes in v1:
time: 121 us
  blocking collectives  50.8 us (42%)
  Pallas kernels  35.4 us (29%)
  waiting for transfers between devices  17.9 us (15%)
  starting transfers between devices  7.63 us (6%)
  local copies, waits for them, and re-layouts  6.96 us (6%)
    all_to_all x3, blocking collectives, exchange(): lax.all_to_all(array, BOTH, 0, 0, tiled=True, axis_index_groups=groups)  50.8 us
    pallas_call x2, Pallas kernels, attention_call(): pl.pallas_call(prior_kernel if prior else own_kernel, out_shape=[jax.Shap...  29.6 us
    ppermute x4, waiting for transfers between devices, from_behind(): lax.ppermute(block, 'seq', [((i - distance) % 8, i) for i in range(8)])  17.9 us
    ppermute x4, starting transfers between devices, from_behind(): lax.ppermute(block, 'seq', [((i - distance) % 8, i) for i in range(8)])  7.63 us
    unnamed x22, local copies, waits for them, and re-layouts  6.04 us
    pallas_call x1, Pallas kernels, shards(): pl.pallas_call(norm_kernel, out_shape=[jax.ShapeDtypeStruct((TOKENS, WIDT...  2.68 us
  transfers between devices with their start and end apart: 4, of which 2 were waited for; matrix products, arithmetic and copies ran while one was open for 0% of the time, Pallas kernels for 10%

profile of v1, /device:TPU:1, one launch (start us, length us, event | category | flops | bytes accessed | tf_op | source)
XLA Modules:
  0.0 120.6 jit_solution(4806822805241831628)
XLA Ops:
  0.6 0.0 copy-start.10
  0.6 0.0 copy-start.8
  0.7 0.0 copy-start.9
  0.7 0.8 reshape.26.scale_ref
  1.4 1.0 pad_maximum_fusion.down_ref
  2.4 0.0 copy-start.2
  2.4 2.2 %copy-done.2 = bf16[1,256,8192]{2,1,0:T(8,128)(2,1)S(1)} copy-done((bf16[1,256,8192]{2,1,0:T(8,128)(2,1)S(1)}, bf16[1,256,8192]{2,1,0:T(8,128)(2,1)}, u32[]{:S(2)}) %copy-start.2) | copy-done | bytes 4194328
  4.6 0.0 copy-start.5
  4.6 2.7 %norm.1 = (bf16[256,8192]{1,0:T(8,128)(2,1)S(1)}, bf16[256,8]{1,0:T(8,128)(2,1)S(1)}, bf16[256,8]{1,0:T(8,128)(2,1)S(1)}, bf16[8,256]{1,0:T(8,128)(2,1)S(1)}, bf16[8,256]{1,0:T(8,128)(2,1)S(1)}) custom-call(bf16[256,8192]{1,0:T(8,128)(2,1)S(1)} %bitcast.8, bf16[1,8192]{1,0:T(2,128)(2,1)S(1)} %reshape.26.scale_ref, bf16[16,8192]{1,0:T(8,128)(2,1)S(1)} %pad_maximum_fusion.down_ref), custom_call_target="tpu_custom_call" | custom-call | tf_op jit(solution)/shard_map/norm/pallas_call | solution.py:335
  7.3 0.0 copy-start
  7.3 1.9 %copy-done = bf16[256,8192]{1,0:T(8,128)(2,1)} copy-done((bf16[256,8192]{1,0:T(8,128)(2,1)}, bf16[256,8192]{1,0:T(8,128)(2,1)S(1)}, u32[]{:S(2)}) %copy-start) | copy-done | bytes 4194328
  9.3 3.6 %collective-permute-start.2 = (bf16[8,256]{1,0:T(8,128)(2,1)S(1)}, bf16[8,256]{1,0:T(8,128)(2,1)S(1)}, u32[]{:S(2)}, u32[]{:S(2)}) collective-permute-start(bf16[8,256]{1,0:T(8,128)(2,1)S(1)} %get-tuple-element.28.vmt_ref), channel_id=1, source_target_pairs={{224,0},{0,32},{32,64},{64,96},{96,128},{128,160},{160,192},{192,2... | collective-permute-start | bytes 12296 | tf_op jit(solution)/shard_map/ppermute | solution.py:263
  12.8 1.2 %collective-permute-start = (bf16[256,768]{1,0:T(8,128)(2,1)}, bf16[256,768]{1,0:T(8,128)(2,1)}, u32[]{:S(2)}, u32[]{:S(2)}) collective-permute-start(bf16[256,768]{1,0:T(8,128)(2,1)} %bitcast.3.k_ref), channel_id=1, source_target_pairs={{224,0},{0,32},{32,64},{64,96},{96,128},{128,160},{160,192},{192,2... | collective-permute-start | bytes 1179656 | tf_op jit(solution)/shard_map/ppermute | solution.py:263
  14.1 2.7 %collective-permute-start.1 = (bf16[256,768]{1,0:T(8,128)(2,1)}, bf16[256,768]{1,0:T(8,128)(2,1)}, u32[]{:S(2)}, u32[]{:S(2)}) collective-permute-start(bf16[256,768]{1,0:T(8,128)(2,1)} %bitcast.4.v_ref), channel_id=1, source_target_pairs={{224,0},{0,32},{32,64},{64,96},{96,128},{128,160},{160,192},{192,2... | collective-permute-start | bytes 1179656 | tf_op jit(solution)/shard_map/ppermute | solution.py:263
  16.8 0.0 copy-done.10
  16.8 0.1 fusion
  16.9 0.1 broadcast_select_fusion.ids_ref
  17.0 0.0 collective-permute-done.2.vmtp_ref
  17.0 9.5 %collective-permute-done.kp_ref = bf16[256,768]{1,0:T(8,128)(2,1)} collective-permute-done((bf16[256,768]{1,0:T(8,128)(2,1)}, bf16[256,768]{1,0:T(8,128)(2,1)}, u32[]{:S(2)}, u32[]{:S(2)}) %collective-permute-start) | collective-permute-done | bytes 393248 | tf_op jit(solution)/shard_map/ppermute | solution.py:263
  26.4 8.4 %collective-permute-done.1.vp_ref = bf16[256,768]{1,0:T(8,128)(2,1)} collective-permute-done((bf16[256,768]{1,0:T(8,128)(2,1)}, bf16[256,768]{1,0:T(8,128)(2,1)}, u32[]{:S(2)}, u32[]{:S(2)}) %collective-permute-start.1) | collective-permute-done | bytes 393248 | tf_op jit(solution)/shard_map/ppermute | solution.py:263
  34.9 0.0 copy-done.8
  34.9 0.0 copy-done.9
  34.9 0.0 copy-done.5
  34.9 0.0 copy-start.6
  34.9 1.9 %copy-done.6 = bf16[1,256,6144]{2,1,0:T(8,128)(2,1)S(1)} copy-done((bf16[1,256,6144]{2,1,0:T(8,128)(2,1)S(1)}, bf16[1,256,6144]{2,1,0:T(8,128)(2,1)}, u32[]{:S(2)}) %copy-start.6) | copy-done | bytes 3145752
  36.8 0.0 copy-start.7
  36.8 17.4 %prior_attention.1 = (f32[3,8,1024]{2,1,0:T(8,128)S(1)}, f32[3,8,128]{2,1,0:T(8,128)S(1)}, f32[8,256]{1,0:T(8,128)S(1)}, f32[8,256]{1,0:T(8,128)S(1)}, f32[8,256]{1,0:T(8,128)S(1)}) custom-call(s32[6]{0:T(128)S(1)} %broadcast_select_fusion.ids_ref, bf16[256,6144]{1,0:T(8,128)(2,1)S(1)} %bitcast.11, bf16[256,6144]{1,0:T(8,128)(2,1)S(1)} %bitcast.13, ...), custom_call_target="tpu_custom_call" | custom-call | flops 6000000000 | bytes 4000000 | tf_op jit(solution)/shard_map/prior_attention/pallas_call | solution.py:286
  54.2 0.0 copy-start.1
  54.2 0.1 collective-permute-start.3
  54.3 0.0 copy-done.7
  54.3 12.2 %own_attention.1 = (f32[3,8,1024]{2,1,0:T(8,128)S(1)}, f32[3,8,128]{2,1,0:T(8,128)S(1)}, f32[8,256]{1,0:T(8,128)S(1)}, f32[8,256]{1,0:T(8,128)S(1)}) custom-call(s32[6]{0:T(128)S(1)} %broadcast_select_fusion.ids_ref, bf16[256,6144]{1,0:T(8,128)(2,1)S(1)} %bitcast.12, bf16[256,6144]{1,0:T(8,128)(2,1)S(1)} %bitcast.14, bf16[256,768]{1,0:T(8,128)(2,1)} %bitcast.3.k_ref, ...), custom_call_target="tpu_custom_call" | custom-call | flops 3000000000 | bytes 4000000 | tf_op jit(solution)/shard_map/own_attention/pallas_call | solution.py:286
  66.5 0.0 copy-start.3
  66.5 0.0 copy-start.4
  66.5 0.0 collective-permute-done.3.dvh_ref
  66.5 0.0 copy-done.1
  66.5 2.0 %gradients.1 = bf16[96,16,128]{2,1,0:T(8,128)(2,1)S(1)} custom-call(s32[6]{0:T(128)S(1)} %broadcast_select_fusion.ids_ref, bf16[256,8192]{1,0:T(8,128)(2,1)S(1)} %copy-done.1, f32[8,256]{1,0:T(8,128)S(1)} %get-tuple-element.29.dqm1_ref, f32[8,256]{1,0:T(8,128)S(1)} %get-tuple-element.30.dqm2_ref, f32[8,256]{1,0:T(8,128)S(1)} %get-tuple-element.31.dvm1_ref, ...), custom_call_target="tpu_custom_call" | custom-call | tf_op jit(solution)/shard_map/gradients/pallas_call | solution.py:369
  68.5 17.8 %all_to_all.15 = bf16[32,3,16,128]{3,2,1,0:T(8,128)(2,1)S(1)} all-to-all(bf16[32,3,16,128]{3,2,1,0:T(8,128)(2,1)S(1)} %bitcast.9), channel_id=1, replica_groups={{0,1,2,3,32,33,34,35,64,65,66,67,96,97,98,99,128,129,130,131,160,161,16..., dimensions={0} | all-to-all | bytes 786432 | tf_op jit(solution)/shard_map/all_to_all | solution.py:250
  86.3 0.1 convert_reduce_fusion
  86.4 17.4 %all_to_all.16 = f32[8,3,16,128]{3,2,1,0:T(8,128)S(1)} all-to-all(f32[8,3,16,128]{3,2,1,0:T(8,128)S(1)} %broadcast_in_dim.4), channel_id=1, replica_groups={{0,4,8,12,16,20,24,28},{1,5,9,13,17,21,25,29},{2,6,10,14,18,22,26,30},{..., dimensions={0} | all-to-all | bytes 393216 | tf_op jit(solution)/shard_map/all_to_all | solution.py:250
  103.8 0.1 broadcast_in_dim.5
  103.9 15.6 %all_to_all.17 = bf16[32,3,16,128]{3,2,1,0:T(8,128)(2,1)S(1)} all-to-all(bf16[32,3,16,128]{3,2,1,0:T(8,128)(2,1)S(1)} %broadcast_in_dim.5), channel_id=1, replica_groups={{0,1,2,3,32,33,34,35,64,65,66,67,96,97,98,99,128,129,130,131,160,161,16..., dimensions={0} | all-to-all | bytes 786432 | tf_op jit(solution)/shard_map/all_to_all | solution.py:250
  119.4 0.0 copy-done.3
  119.4 0.0 copy-done.4
  119.4 1.2 clip.1
  (2 shorter events, 0.0 us)
Async XLA Ops:
  0.6 16.2 %copy-start.10 = (s32[6]{0:T(128)S(1)}, s32[6]{0:T(128)}, u32[]{:S(2)}) copy-start(s32[6]{0:T(128)} %param.21) | copy-start | bytes 76
  0.6 34.2 %copy-start.8 = (bf16[8,6144]{1,0:T(8,128)(2,1)S(1)}, bf16[8,6144]{1,0:T(8,128)(2,1)}, u32[]{:S(2)}) copy-start(bf16[8,6144]{1,0:T(8,128)(2,1)} %qup_ref.3) | copy-start | bytes 294916
  0.7 34.2 %copy-start.9 = (bf16[8,768]{1,0:T(8,128)(2,1)S(1)}, bf16[8,768]{1,0:T(8,128)(2,1)}, u32[]{:S(2)}) copy-start(bf16[8,768]{1,0:T(8,128)(2,1)} %vup_ref.3) | copy-start | bytes 36868
  2.4 2.2 %copy-start.2 = (bf16[1,256,8192]{2,1,0:T(8,128)(2,1)S(1)}, bf16[1,256,8192]{2,1,0:T(8,128)(2,1)}, u32[]{:S(2)}) copy-start(bf16[1,256,8192]{2,1,0:T(8,128)(2,1)} %param.11) | copy-start | bytes 12582916
  4.6 30.2 %copy-start.5 = (bf16[1,256,6144]{2,1,0:T(8,128)(2,1)S(1)}, bf16[1,256,6144]{2,1,0:T(8,128)(2,1)}, u32[]{:S(2)}) copy-start(bf16[1,256,6144]{2,1,0:T(8,128)(2,1)} %param.12) | copy-start | bytes 9437188
  7.3 1.9 %copy-start = (bf16[256,8192]{1,0:T(8,128)(2,1)}, bf16[256,8192]{1,0:T(8,128)(2,1)S(1)}, u32[]{:S(2)}) copy-start(bf16[256,8192]{1,0:T(8,128)(2,1)S(1)} %get-tuple-element.24.normed_ref) | copy-start | bytes 12582916
  9.3 7.7 %collective-permute-start.2 = (bf16[8,256]{1,0:T(8,128)(2,1)S(1)}, bf16[8,256]{1,0:T(8,128)(2,1)S(1)}, u32[]{:S(2)}, u32[]{:S(2)}) collective-permute-start(bf16[8,256]{1,0:T(8,128)(2,1)S(1)} %get-tuple-element.28.vmt_ref), channel_id=1, source_target_pairs={{224,0},{0,32},{32,64},{64,96},{96,128},{128,160},{160,192},{192,2... | collective-permute-start | bytes 12296 | tf_op jit(solution)/shard_map/ppermute | solution.py:263
  12.8 13.6 %collective-permute-start = (bf16[256,768]{1,0:T(8,128)(2,1)}, bf16[256,768]{1,0:T(8,128)(2,1)}, u32[]{:S(2)}, u32[]{:S(2)}) collective-permute-start(bf16[256,768]{1,0:T(8,128)(2,1)} %bitcast.3.k_ref), channel_id=1, source_target_pairs={{224,0},{0,32},{32,64},{64,96},{96,128},{128,160},{160,192},{192,2... | collective-permute-start | bytes 1179656 | tf_op jit(solution)/shard_map/ppermute | solution.py:263
  14.1 20.8 %collective-permute-start.1 = (bf16[256,768]{1,0:T(8,128)(2,1)}, bf16[256,768]{1,0:T(8,128)(2,1)}, u32[]{:S(2)}, u32[]{:S(2)}) collective-permute-start(bf16[256,768]{1,0:T(8,128)(2,1)} %bitcast.4.v_ref), channel_id=1, source_target_pairs={{224,0},{0,32},{32,64},{64,96},{96,128},{128,160},{160,192},{192,2... | collective-permute-start | bytes 1179656 | tf_op jit(solution)/shard_map/ppermute | solution.py:263
  34.9 1.9 %copy-start.6 = (bf16[1,256,6144]{2,1,0:T(8,128)(2,1)S(1)}, bf16[1,256,6144]{2,1,0:T(8,128)(2,1)}, u32[]{:S(2)}) copy-start(bf16[1,256,6144]{2,1,0:T(8,128)(2,1)} %param.15) | copy-start | bytes 9437188
  36.8 17.5 %copy-start.7 = (bf16[1,256,6144]{2,1,0:T(8,128)(2,1)S(1)}, bf16[1,256,6144]{2,1,0:T(8,128)(2,1)}, u32[]{:S(2)}) copy-start(bf16[1,256,6144]{2,1,0:T(8,128)(2,1)} %param.15) | copy-start | bytes 9437188
  54.2 12.3 %copy-start.1 = (bf16[256,8192]{1,0:T(8,128)(2,1)S(1)}, bf16[256,8192]{1,0:T(8,128)(2,1)}, u32[]{:S(2)}) copy-start(bf16[256,8192]{1,0:T(8,128)(2,1)} %copy-done) | copy-start | bytes 12582916
  54.2 12.3 %collective-permute-start.3 = (f32[8,256]{1,0:T(8,128)S(1)}, f32[8,256]{1,0:T(8,128)S(1)}, u32[]{:S(2)}, u32[]{:S(2)}) collective-permute-start(f32[8,256]{1,0:T(8,128)S(1)} %get-tuple-element.33), channel_id=1, source_target_pairs={{32,0},{64,32},{96,64},{128,96},{160,128},{192,160},{224,192},{0,2... | collective-permute-start | bytes 24584 | tf_op jit(solution)/shard_map/ppermute | solution.py:263
  66.5 53.0 %copy-start.3 = (bf16[8,8192]{1,0:T(8,128)(2,1)S(1)}, bf16[8,8192]{1,0:T(8,128)(2,1)}, u32[]{:S(2)}) copy-start(bf16[8,8192]{1,0:T(8,128)(2,1)} %vd_ref.1) | copy-start | bytes 393220
  66.5 53.0 %copy-start.4 = (bf16[8,8192]{1,0:T(8,128)(2,1)S(1)}, bf16[8,8192]{1,0:T(8,128)(2,1)}, u32[]{:S(2)}) copy-start(bf16[8,8192]{1,0:T(8,128)(2,1)} %qd_ref.1) | copy-start | bytes 393220

commit v2 on v1

v2 whole, which is shorter than its diff:
```python
import functools
import math

import jax
import jax.numpy as jnp
from jax import lax
from jax.experimental import pallas as pl
from jax.experimental.pallas import tpu as pltpu
from jax.sharding import PartitionSpec as P

HEAD_SIZE = 128
TOKENS = 256
HALF = 128
WIDTH = 8192
RANK = 8
KV_HEADS = 6
SHARE = 8
LANES = SHARE * HEAD_SIZE
EPS = 1e-05
FACTOR = 1.0 / math.sqrt(HEAD_SIZE)
LOG2_E = 1.4426950408889634
TILES = 96
QB_TILE = 64
F32 = jnp.float32
BF16 = jnp.bfloat16
BOTH = ("seq", "dp")
MIB = 1024 * 1024


def nn(left, right):
    return jnp.dot(left, right, preferred_element_type=F32)


def nt(left, right):
    return lax.dot_general(left, right, (((1,), (1,)), ((), ())), preferred_element_type=F32)


def norm_kernel(x_ref, down_ref, normed_ref, qm_ref, vm_ref, qmt_ref, vmt_ref):
    step = 1024
    total = jnp.zeros((HALF, HEAD_SIZE), F32)
    for start in range(0, WIDTH, HEAD_SIZE):
        part = x_ref[:, start : start + HEAD_SIZE].astype(F32)
        total = total + part * part
    mean = jnp.sum(total, axis=1, keepdims=True) * (1.0 / WIDTH)
    inverse = lax.rsqrt(mean + EPS)
    mid = jnp.zeros((HALF, 2 * RANK), F32)
    for start in range(0, WIDTH, step):
        cols = slice(start, start + step)
        down = down_ref[:, cols]
        unit = x_ref[:, cols].astype(F32) * inverse
        normed = (unit * down[16:32].astype(F32)[:1]).astype(BF16)
        normed_ref[:, cols] = normed
        mid = mid + nt(normed, down[:16])
    qm_ref[...] = mid[:, :RANK].astype(BF16)
    vm_ref[...] = mid[:, RANK:].astype(BF16)
    mid_t = mid.T
    qmt_ref[...] = mid_t[:RANK].astype(BF16)
    vmt_ref[...] = mid_t[RANK:].astype(BF16)


def pick_kernel(ids_ref, k_ref, v_ref, vm_ref, vmt_ref, vup_ref, keys_ref, values_ref):
    for i in range(3):
        small = head_cols(ids_ref, 3 + i, HEAD_SIZE)
        keys_ref[i] = k_ref[:, small]
        values_ref[i] = adapted(v_ref[:, small], vm_ref[...], vup_ref[:, small])
    mid_t = vmt_ref[...].astype(F32)
    pad = jnp.zeros((RANK, HEAD_SIZE), F32)
    values_ref[3] = jnp.zeros((TOKENS, HEAD_SIZE), BF16)
    for j in range(2):
        block = jnp.concatenate([mid_t[:, j * HEAD_SIZE : (j + 1) * HEAD_SIZE], pad], axis=0)
        values_ref[3, j * 16 : (j + 1) * 16] = block.astype(BF16)


def head_at(ids_ref, place):
    odd = lax.axis_index("seq") % 2
    return jnp.where(odd == 1, ids_ref[(place + 3) % KV_HEADS], ids_ref[place])


def head_cols(ids_ref, place, size):
    return pl.ds(pl.multiple_of(head_at(ids_ref, place) * size, size), size)


def token_rows(c):
    return slice(c * HALF, (c + 1) * HALF)


def stacked(ref, i, c):
    return jnp.concatenate(
        [ref[i, token_rows(c), j * HEAD_SIZE : (j + 1) * HEAD_SIZE] for j in range(SHARE)], axis=0
    )


def stacked_grads(ref, ids_ref, place, c):
    start = head_at(ids_ref, place) * LANES
    return jnp.concatenate(
        [
            ref[token_rows(c), pl.ds(pl.multiple_of(start + j * HEAD_SIZE, HEAD_SIZE), HEAD_SIZE)]
            for j in range(SHARE)
        ],
        axis=0,
    )


def causal_mask():
    key_id = lax.broadcasted_iota(jnp.int32, (HALF, HALF), 0)
    query_id = lax.broadcasted_iota(jnp.int32, (HALF, HALF), 1)
    return jnp.concatenate([key_id <= query_id] * SHARE, axis=1)


def transposed(array):
    return array.astype(F32).T.astype(BF16)


def adapted(frozen, mid, up):
    return (frozen.astype(F32) + 2.0 * nn(mid, up)).astype(BF16)


def own_scores(keys, queries, c, mask):
    own = nt(keys[: (c + 1) * HALF], queries) * (FACTOR * LOG2_E)
    if c == 0:
        return [jnp.where(mask, own, -jnp.inf)]
    return [own[:HALF], jnp.where(mask, own[HALF:], -jnp.inf)]


def softmax(parts):
    top = functools.reduce(jnp.maximum, [jnp.max(s, axis=0, keepdims=True) for s in parts])
    exps = [jnp.exp2(s - top) for s in parts]
    denom = functools.reduce(jnp.add, [jnp.sum(e, axis=0, keepdims=True) for e in exps])
    inv = 1.0 / denom
    return [e * inv for e in exps]


def summed_over_keys(parts):
    return functools.reduce(jnp.add, [jnp.sum(p, axis=0, keepdims=True) for p in parts])


def keep_dq(dq_scr, i, c, dq_t):
    dq_b = (dq_t * FACTOR).astype(BF16)
    for j in range(SHARE):
        dq_scr[i, j * HEAD_SIZE : (j + 1) * HEAD_SIZE, token_rows(c)] = dq_b[:, j * HALF : (j + 1) * HALF]


UNITS = [(i, c) for i in range(3) for c in range(2)]


def pipelined(before, after):
    ahead = before(*UNITS[0])
    for n, unit in enumerate(UNITS):
        state, ahead = ahead, before(*UNITS[n + 1]) if n + 1 < len(UNITS) else None
        after(*unit, state)


def own_kernel(
    ids_ref, q_ref, g_ref, k_ref, v_ref, qm_ref, vm_ref, qmt_ref, vmt_ref, qup_ref, vup_ref,
    qb_ref, vb_ref, dqm_ref, dvm_ref, q_scr, dq_scr,
):
    mask = causal_mask()
    heads = {}
    totals = {}

    def before(i, c):
        if c == 0:
            small = head_cols(ids_ref, 3 + i, HEAD_SIZE)
            keys = k_ref[:, small]
            vup, qup = vup_ref[:, small], qup_ref[:, head_cols(ids_ref, 3 + i, LANES)]
            q_scr[i] = adapted(q_ref[:, head_cols(ids_ref, 3 + i, LANES)], qm_ref[...], qup)
            heads[i] = (keys, transposed(keys), adapted(v_ref[:, small], vm_ref[...], vup), qup, vup)
        keys, _, values, _, _ = heads[i]
        grads = stacked_grads(g_ref, ids_ref, 3 + i, c)
        return own_scores(keys, stacked(q_scr, i, c), c, mask), nt(values[: (c + 1) * HALF], grads), grads

    def after(i, c, state):
        parts, dprob, grads = state
        _, keys_t, _, qup, vup = heads[i]
        probs = softmax(parts)
        dprobs = [dprob[j * HALF : (j + 1) * HALF] for j in range(c + 1)]
        weights = [p.astype(BF16) for p in probs]
        delta = summed_over_keys([w.astype(F32) * d for w, d in zip(weights, dprobs)])
        dscore = [(p * (d - delta)).astype(BF16) for p, d in zip(probs, dprobs)]
        near = (c + 1) * HALF
        keep_dq(dq_scr, i, c, nn(keys_t[:, :near], jnp.concatenate(dscore, axis=0)))
        term = nn(jnp.concatenate(weights, axis=0), grads)
        if c == 0:
            totals["low"] = term
            return
        dv = jnp.concatenate([totals["low"] + term[:HALF], term[HALF:]], axis=0).astype(BF16)
        dq_t = dq_scr[i]
        qb_ref[i] = 2.0 * nt(qmt_ref[...], dq_t)
        vb_ref[i] = 2.0 * nn(vmt_ref[...], dv)
        dq, dv = 2.0 * nn(qup, dq_t), 2.0 * nt(vup, dv)
        totals["dq"] = totals["dq"] + dq if i else dq
        totals["dv"] = totals["dv"] + dv if i else dv

    pipelined(before, after)
    dqm_ref[...] = totals["dq"]
    dvm_ref[...] = totals["dv"]


def weights_kernel(
    ids_ref, q_ref, g_ref, k_ref, qm_ref, vmt_ref, qup_ref, vup_ref, kp_ref, dvm1_ref,
    w_ref, dvp_ref, vb_ref, dvm_ref, handed_ref, q_scr,
):
    mask = causal_mask()
    heads = {}
    totals = {"dv": dvm1_ref[...]}

    def before(i, c):
        if c == 0:
            small = head_cols(ids_ref, i, HEAD_SIZE)
            qup = qup_ref[:, head_cols(ids_ref, i, LANES)]
            q_scr[i] = adapted(q_ref[:, head_cols(ids_ref, i, LANES)], qm_ref[...], qup)
            heads[i] = (k_ref[:, small], kp_ref[i], vup_ref[:, small])
        keys, prior, _ = heads[i]
        queries = stacked(q_scr, i, c)
        return own_scores(keys, queries, c, mask), nt(prior, queries) * (FACTOR * LOG2_E)

    def after(i, c, state):
        own, prior = state
        probs = softmax(own + [prior])
        weights = jnp.concatenate([p.astype(BF16) for p in probs], axis=0)
        rows = 3 * HALF + c * HALF
        w_ref[i, c * 3 * HALF : c * 3 * HALF + rows] = weights
        grads = stacked_grads(g_ref, ids_ref, i, c)
        term = nn(weights, grads)
        if c == 0:
            totals["low"] = term
            return
        low = totals["low"]
        dv = jnp.concatenate([low[:HALF] + term[:HALF], term[HALF : 2 * HALF]], axis=0).astype(BF16)
        dv_prior = (low[HALF:] + term[2 * HALF :]).astype(BF16)
        _, _, vup = heads[i]
        dvp_ref[i] = dv_prior
        vb_ref[i] = 2.0 * nn(vmt_ref[...], dv)
        totals["dv"] = totals["dv"] + 2.0 * nt(vup, dv)
        handed = 2.0 * nt(vup, dv_prior)
        totals["handed"] = totals["handed"] + handed if i else handed

    pipelined(before, after)
    dvm_ref[...] = totals["dv"]
    handed_ref[...] = totals["handed"]


def dscore_kernel(
    ids_ref, g_ref, k_ref, v_ref, vm_ref, qmt_ref, qup_ref, vup_ref, kp_ref, vp_ref,
    w_ref, dvp_ref, vb1_ref, dqm1_ref, qb_ref, vb_ref, dqm_ref, dq_scr,
):
    vmt_prior = jnp.concatenate(
        [vp_ref[3, j * 16 : (j + 1) * 16].astype(F32)[:RANK] for j in range(2)], axis=1
    ).astype(BF16)
    heads = {}
    totals = {"dq": dqm1_ref[...]}

    def before(i, c):
        if c == 0:
            small = head_cols(ids_ref, i, HEAD_SIZE)
            vup = vup_ref[:, small]
            heads[i] = (
                transposed(k_ref[:, small]),
                transposed(kp_ref[i]),
                adapted(v_ref[:, small], vm_ref[...], vup),
                vp_ref[i],
            )
        _, _, values, prior = heads[i]
        grads = stacked_grads(g_ref, ids_ref, i, c)
        return nt(values[: (c + 1) * HALF], grads), nt(prior, grads)

    def after(i, c, dprobs):
        keys_t, prior_t, _, _ = heads[i]
        near = (c + 1) * HALF
        start = c * 3 * HALF
        weights = [
            w_ref[i, start : start + near].astype(F32),
            w_ref[i, start + near : start + near + TOKENS].astype(F32),
        ]
        delta = summed_over_keys([w * d for w, d in zip(weights, dprobs)])
        dscore = [(w * (d - delta)).astype(BF16) for w, d in zip(weights, dprobs)]
        keep_dq(dq_scr, i, c, nn(keys_t[:, :near], dscore[0]) + nn(prior_t, dscore[1]))
        if c == 0:
            return
        dq_t = dq_scr[i]
        qb_ref[i] = 2.0 * nt(qmt_ref[...], dq_t)
        vb_ref[i] = vb1_ref[i] + 2.0 * nn(vmt_prior, dvp_ref[i])
        totals["dq"] = totals["dq"] + 2.0 * nn(qup_ref[:, head_cols(ids_ref, i, LANES)], dq_t)

    pipelined(before, after)
    dqm_ref[...] = totals["dq"]


def gather_kernel(
    ids_ref, normed_ref, dqm_ref, dvm_ref, dvh_ref,
    qb1_ref, vb1_ref, qb2_ref, vb2_ref, out_ref, buf,
):
    step = pl.program_id(0)

    @pl.when(step < 4)
    def _():
        dq = dqm_ref[...]
        dv = dvm_ref[...] + dvh_ref[...]
        mids = jnp.concatenate([dq, dv], axis=0).astype(BF16)
        for j in range(4):
            part = nn(mids, normed_ref[:, j * 512 : (j + 1) * 512]).astype(BF16)
            for k in range(4):
                out_ref[4 * j + k] = part[:, k * HEAD_SIZE : (k + 1) * HEAD_SIZE]

    @pl.when(step == 4)
    def _():
        buf[27:32] = jnp.zeros((5, 16, HEAD_SIZE), F32)
        for i in range(3):
            for base, qb_ref, vb_ref in ((0, qb2_ref, vb2_ref), (3, qb1_ref, vb1_ref)):
                head = head_at(ids_ref, base + i)
                upper = head >= 3
                row = pl.multiple_of(jnp.where(upper, 8, 0), 8)
                place = jnp.where(upper, head - 3, head)
                for k in range(SHARE):
                    buf[place * SHARE + k, pl.ds(row, 8), :] = qb_ref[i][:, k * HEAD_SIZE : (k + 1) * HEAD_SIZE]
                buf[24 + place, pl.ds(row, 8), :] = vb_ref[i]
        for t in range(16):
            out_ref[t] = buf[t].astype(BF16)

    @pl.when(step == 5)
    def _():
        for t in range(16):
            out_ref[t] = buf[16 + t].astype(BF16)


def clip_kernel(limit, sum_ref, qd_ref, vd_ref, scale_ref, qa_ref, qb_ref, va_ref, vb_ref, gain_ref, gains):
    total = jnp.zeros((16, HEAD_SIZE), F32)
    gain_total = jnp.zeros((1, HEAD_SIZE), F32)
    for t in range(QB_TILE):
        cols = slice(t * HEAD_SIZE, (t + 1) * HEAD_SIZE)
        tile = sum_ref[t].astype(F32)
        total = total + tile * tile
        mixed = qd_ref[:, cols].astype(F32) * tile[:RANK] + vd_ref[:, cols].astype(F32) * tile[RANK:]
        gain = jnp.sum(mixed, axis=0, keepdims=True) / scale_ref[:, cols].astype(F32)
        gains[:, cols] = gain
        gain_total = gain_total + gain * gain
    for t in range(QB_TILE, QB_TILE + 27):
        tile = sum_ref[t].astype(F32)
        total = total + tile * tile
    squares = jnp.sum(total, keepdims=True) + jnp.sum(gain_total, keepdims=True)
    factor = jnp.minimum(1.0, limit / jnp.sqrt(squares))
    gain_ref[...] = gains[...] * factor
    for t in range(QB_TILE):
        cols = slice(t * HEAD_SIZE, (t + 1) * HEAD_SIZE)
        tile = sum_ref[t].astype(F32) * factor
        qa_ref[:, cols] = tile[:RANK]
        va_ref[:, cols] = tile[RANK:]
    for t in range(24):
        tile = sum_ref[QB_TILE + t].astype(F32) * factor
        qb_ref[:, t * HEAD_SIZE : (t + 1) * HEAD_SIZE] = tile[:RANK]
        qb_ref[:, (24 + t) * HEAD_SIZE : (25 + t) * HEAD_SIZE] = tile[RANK:]
    for t in range(3):
        tile = sum_ref[QB_TILE + 24 + t].astype(F32) * factor
        vb_ref[:, t * HEAD_SIZE : (t + 1) * HEAD_SIZE] = tile[:RANK]
        vb_ref[:, (3 + t) * HEAD_SIZE : (4 + t) * HEAD_SIZE] = tile[RANK:]


def groups_along(keys):
    found = {}
    for device in range(256):
        y, xh, z, rest = device // 64, device // 32 % 2, device // 4 % 8, device % 4
        place = {"y": y, "xh": xh, "z": z, "xl": rest // 2, "core": rest % 2}
        found.setdefault(tuple(v for k, v in place.items() if k not in keys), []).append(device)
    return list(found.values())


PLANE = groups_along(("y", "xh", "xl", "core"))
COLUMN = groups_along(("z",))


def exchange(array, groups):
    return lax.all_to_all(array, BOTH, 0, 0, tiled=True, axis_index_groups=groups)


def sum_over_devices(tiles):
    shares = tiles.reshape(32, 3, 16, HEAD_SIZE)
    mine = jnp.sum(exchange(shares, PLANE).astype(F32), axis=0).astype(BF16)
    copies = jnp.broadcast_to(mine[None], (8, 3, 16, HEAD_SIZE))
    mine = jnp.sum(exchange(copies, COLUMN).astype(F32), axis=0).astype(BF16)
    copies = jnp.broadcast_to(mine[None], (32, 3, 16, HEAD_SIZE))
    return exchange(copies, PLANE).reshape(TILES, 16, HEAD_SIZE)


def from_behind(block, distance):
    return lax.ppermute(block, "seq", [((i - distance) % 8, i) for i in range(8)])


def whole(shape):
    return pl.BlockSpec(shape, lambda *_: (0,) * len(shape))


def params(mib):
    return pltpu.CompilerParams(vmem_limit_bytes=mib * MIB)


def struct(shape, dtype):
    return jax.ShapeDtypeStruct(shape, dtype)


VMEM = pl.BlockSpec(memory_space=pltpu.VMEM)
SMEM = pl.BlockSpec(memory_space=pltpu.SMEM)
HBM = pl.BlockSpec(memory_space=pl.ANY)


def cost(us):
    return pl.CostEstimate(flops=int(us * 1e9), bytes_accessed=0, transcendentals=0)


def own_call(ids, q, g, k, v, qm, vm, qmt, vmt, qup, vup):
    return pl.pallas_call(
        own_kernel,
        out_shape=[
            struct((3, RANK, LANES), F32), struct((3, RANK, HEAD_SIZE), F32),
            struct((RANK, TOKENS), F32), struct((RANK, TOKENS), F32),
        ],
        in_specs=[SMEM] + [VMEM] * 10,
        out_specs=[VMEM] * 4,
        scratch_shapes=[pltpu.VMEM((3, TOKENS, LANES), BF16), pltpu.VMEM((3, LANES, TOKENS), BF16)],
        compiler_params=params(28),
        cost_estimate=cost(1),
        name="own_attention",
    )(ids, q, g, k, v, qm, vm, qmt, vmt, qup, vup)


def weights_call(ids, q, g, k, qm, vmt, qup, vup, kv_prior, dvm):
    return pl.pallas_call(
        weights_kernel,
        out_shape=[
            struct((3, 7 * HALF, LANES), BF16), struct((3, TOKENS, HEAD_SIZE), BF16),
            struct((3, RANK, HEAD_SIZE), F32), struct((RANK, TOKENS), F32), struct((RANK, TOKENS), F32),
        ],
        in_specs=[SMEM] + [VMEM] * 9,
        out_specs=[VMEM] * 5,
        scratch_shapes=[pltpu.VMEM((3, TOKENS, LANES), BF16)],
        compiler_params=params(32),
        cost_estimate=cost(4),
        name="prior_weights",
    )(ids, q, g, k, qm, vmt, qup, vup, kv_prior, dvm)


def dscore_call(ids, g, k, v, vm, qmt, qup, vup, kv_prior, vmt_prior, w, dvp, vb, dqm):
    return pl.pallas_call(
        dscore_kernel,
        out_shape=[
            struct((3, RANK, LANES), F32), struct((3, RANK, HEAD_SIZE), F32), struct((RANK, TOKENS), F32),
        ],
        in_specs=[SMEM] + [VMEM] * 13,
        out_specs=[VMEM] * 3,
        scratch_shapes=[pltpu.VMEM((3, LANES, TOKENS), BF16)],
        compiler_params=params(32),
        cost_estimate=cost(4),
        name="prior_dscore",
    )(ids, g, k, v, vm, qmt, qup, vup, kv_prior, vmt_prior, w, dvp, vb, dqm)


def shards(
    layer_input,
    frozen_queries,
    frozen_keys,
    frozen_values,
    output_gradient,
    norm_scale_vector,
    query_down_weight,
    query_up_weight,
    value_down_weight,
    value_up_weight,
    head_ordering,
):
    x, q, k, v, g = (
        a[0] for a in (layer_input, frozen_queries, frozen_keys, frozen_values, output_gradient)
    )
    ids, qup, vup = head_ordering, query_up_weight, value_up_weight
    scale = norm_scale_vector.reshape(1, WIDTH)
    down = jnp.concatenate(
        [query_down_weight, value_down_weight, jnp.broadcast_to(scale, (16, WIDTH))], axis=0
    )

    normed, qm, vm, qmt, vmt = pl.pallas_call(
        norm_kernel,
        out_shape=[
            struct((TOKENS, WIDTH), BF16), struct((TOKENS, RANK), BF16), struct((TOKENS, RANK), BF16),
            struct((RANK, TOKENS), BF16), struct((RANK, TOKENS), BF16),
        ],
        grid=(2,),
        in_specs=[pl.BlockSpec((HALF, WIDTH), lambda i: (i, 0)), whole((32, WIDTH))],
        out_specs=[
            pl.BlockSpec((HALF, WIDTH), lambda i: (i, 0)),
            pl.BlockSpec((HALF, RANK), lambda i: (i, 0)),
            pl.BlockSpec((HALF, RANK), lambda i: (i, 0)),
            pl.BlockSpec((RANK, HALF), lambda i: (0, i)),
            pl.BlockSpec((RANK, HALF), lambda i: (0, i)),
        ],
        compiler_params=params(20),
        cost_estimate=cost(5),
        name="norm",
    )(x, down)

    keys_out, values_out = pl.pallas_call(
        pick_kernel,
        out_shape=[struct((3, TOKENS, HEAD_SIZE), BF16), struct((4, TOKENS, HEAD_SIZE), BF16)],
        in_specs=[SMEM] + [VMEM] * 5,
        out_specs=[VMEM] * 2,
        compiler_params=params(8),
        name="pick",
    )(ids, k, v, vm, vmt, vup)
    keys_prior = from_behind(keys_out, 1)
    values_prior = from_behind(values_out, 1)

    qb1, vb1, dqm1, dvm1 = own_call(ids, q, g, k, v, qm, vm, qmt, vmt, qup, vup)
    w, dvp, vbp, dvm, handed = weights_call(ids, q, g, k, qm, vmt, qup, vup, keys_prior, dvm1)
    handed = from_behind(handed, -1)
    qb2, vb2, dqm = dscore_call(
        ids, g, k, v, vm, qmt, qup, vup, keys_prior, values_prior, w, dvp, vbp, dqm1
    )

    tiles = pl.pallas_call(
        gather_kernel,
        out_shape=jax.ShapeDtypeStruct((TILES, 16, HEAD_SIZE), BF16),
        grid_spec=pltpu.PrefetchScalarGridSpec(
            num_scalar_prefetch=1,
            grid=(6,),
            in_specs=[pl.BlockSpec((TOKENS, 2048), lambda i, ids: (0, jnp.minimum(i, 3)))]
            + [whole((RANK, TOKENS))] * 3
            + [whole((3, RANK, LANES)), whole((3, RANK, HEAD_SIZE))] * 2,
            out_specs=pl.BlockSpec((16, 16, HEAD_SIZE), lambda i, ids: (i, 0, 0)),
            scratch_shapes=[pltpu.VMEM((32, 16, HEAD_SIZE), F32)],
        ),
        compiler_params=params(16),
        name="gradients",
    )(ids, normed, dqm, dvm, handed, qb1, vb1, qb2, vb2)

    summed = sum_over_devices(tiles)

    listed_items = RANK * (2 * WIDTH + KV_HEADS * LANES + KV_HEADS * HEAD_SIZE) + WIDTH
    qa, qb, va, vb, gain = pl.pallas_call(
        functools.partial(clip_kernel, math.sqrt(listed_items)),
        out_shape=[
            jax.ShapeDtypeStruct((RANK, WIDTH), F32),
            jax.ShapeDtypeStruct((RANK, KV_HEADS * LANES), F32),
            jax.ShapeDtypeStruct((RANK, WIDTH), F32),
            jax.ShapeDtypeStruct((RANK, KV_HEADS * HEAD_SIZE), F32),
            jax.ShapeDtypeStruct((1, WIDTH), F32),
        ],
        scratch_shapes=[pltpu.VMEM((1, WIDTH), F32)],
        compiler_params=params(16),
        name="clip",
    )(summed, query_down_weight, value_down_weight, scale)
    return (qa, qb, va, vb, gain.reshape(WIDTH))


def solution(mesh):
    placed = P("dp", "seq", None)
    return jax.shard_map(
        shards,
        mesh=mesh,
        in_specs=(placed,) * 5 + (P(),) * 6,
        out_specs=(P(), P(), P(), P(), P()),
        check_vma=False,
    )
```

time: 121 us -> 87.1 us (0.72)
  blocking collectives: 50.8 us -> 30.8 us
  Pallas kernels: 35.4 us -> 25.5 us
  waiting for transfers between devices: 17.9 us -> 10.3 us
  starting transfers between devices: 7.63 us -> 14.5 us
  local copies, waits for them, and re-layouts: 6.96 us -> 3.83 us
    all_to_all x3 -> x2, blocking collectives: 50.8 us -> 30.8 us  [exchange(): lax.all_to_all(array, BOTH, 0, 0, tiled=True, axis_index_groups=groups)]
    ppermute x4 -> x3, waiting for transfers between devices: 17.9 us -> 0.01 us  [from_behind(): lax.ppermute(block, 'seq', [((i - distance) % 8, i) for i in range(8)])]
    all_to_all x0 -> x1, waiting for transfers between devices: none -> 10.2 us  [exchange(): lax.all_to_all(array, BOTH, 0, 0, tiled=True, axis_index_groups=groups)]
    pallas_call x3 -> x5, Pallas kernels: 32.3 us -> 22.3 us  [the longest x1 7.13 us: weights_call(): pl.pallas_call(weights_kernel, out_shape=[struct((3, 7 * HALF, LANES), BF...]
    all_to_all x0 -> x1, starting transfers between devices: none -> 5.52 us  [exchange(): lax.all_to_all(array, BOTH, 0, 0, tiled=True, axis_index_groups=groups)]
    unnamed x22, local copies, waits for them, and re-layouts: 6.04 us -> 2.24 us
    ppermute x4 -> x3, starting transfers between devices: 7.63 us -> 8.98 us  [from_behind(): lax.ppermute(block, 'seq', [((i - distance) % 8, i) for i in range(8)])]
  transfers between devices with their start and end apart: 4 -> 4, of which waited for: 2 -> 1; matrix products, arithmetic and copies ran while one was open for 0% -> 0% of each run, Pallas kernels for 10% -> 22%
where the time goes in v2:
time: 87.1 us; the launch traced here: 86.7 us
  blocking collectives  30.8 us (35%)
  Pallas kernels  25.5 us (29%)
  starting transfers between devices  14.5 us (17%)
  waiting for transfers between devices  10.3 us (12%)
  local copies, waits for them, and re-layouts  3.83 us (4%)
  other arithmetic  1.1 us (1%)
    all_to_all x2, blocking collectives, exchange(): lax.all_to_all(array, BOTH, 0, 0, tiled=True, axis_index_groups=groups)  30.8 us
    all_to_all x1, waiting for transfers between devices, exchange(): lax.all_to_all(array, BOTH, 0, 0, tiled=True, axis_index_groups=groups)  10.2 us
    ppermute x3, starting transfers between devices, from_behind(): lax.ppermute(block, 'seq', [((i - distance) % 8, i) for i in range(8)])  8.98 us
    pallas_call x1, Pallas kernels, weights_call(): pl.pallas_call(weights_kernel, out_shape=[struct((3, 7 * HALF, LANES), BF...  7.13 us
    pallas_call x1, Pallas kernels, own_call(): pl.pallas_call(own_kernel, out_shape=[struct((3, RANK, LANES), F32), stru...  5.89 us
    pallas_call x1, Pallas kernels, dscore_call(): pl.pallas_call(dscore_kernel, out_shape=[struct((3, RANK, LANES), F32), s...  5.84 us
    all_to_all x1, starting transfers between devices, exchange(): lax.all_to_all(array, BOTH, 0, 0, tiled=True, axis_index_groups=groups)  5.52 us
    pallas_call x1, Pallas kernels, shards(): pl.pallas_call(norm_kernel, out_shape=[struct((TOKENS, WIDTH), BF16), str...  2.7 us
  transfers between devices with their start and end apart: 4, of which 1 were waited for; matrix products, arithmetic and copies ran while one was open for 0% of the time, Pallas kernels for 22%

profile of v2, /device:TPU:1, one launch (start us, length us, event | category | flops | bytes accessed | tf_op | source)
XLA Modules:
  0.0 86.7 jit_solution(3110806523290153123)
XLA Ops:
  0.6 0.7 broadcast_in_dim.6
  1.4 1.0 %pad_maximum_fusion.down_ref = bf16[32,8192]{1,0:T(8,128)(2,1)S(1)} fusion(bf16[16,8192]{1,0:T(8,128)(2,1)S(1)} %broadcast_in_dim.6, bf16[8,8192]{1,0:T(8,128)(2,1)} %vd_ref.1, bf16[8,8192]{1,0:T(8,128)(2,1)} %qd_ref.1), kind=kLoop, calls=%fused_computation | loop fusion | flops 1572864 | bytes 1048576 | tf_op jit(solution)/shard_map/concatenate | solution.py:474
  2.4 0.0 copy-start.9
  2.4 2.2 %copy-done.9 = bf16[1,256,8192]{2,1,0:T(8,128)(2,1)S(1)} copy-done((bf16[1,256,8192]{2,1,0:T(8,128)(2,1)S(1)}, bf16[1,256,8192]{2,1,0:T(8,128)(2,1)}, u32[]{:S(2)}) %copy-start.9) | copy-done | bytes 4194328
  4.6 0.0 copy-start.2
  4.6 0.0 copy-start.3
  4.6 0.0 copy-start.7
  4.6 0.0 copy-start.8
  4.6 0.0 copy-start
  4.6 0.0 copy-start.1
  4.6 0.0 copy-start.6
  4.6 2.7 %norm.1 = (bf16[256,8192]{1,0:T(8,128)(2,1)S(1)}, bf16[256,8]{1,0:T(8,128)(2,1)S(1)}, bf16[256,8]{1,0:T(8,128)(2,1)S(1)}, bf16[8,256]{1,0:T(8,128)(2,1)S(1)}, bf16[8,256]{1,0:T(8,128)(2,1)S(1)}) custom-call(bf16[256,8192]{1,0:T(8,128)(2,1)S(1)} %bitcast.22, bf16[32,8192]{1,0:T(8,128)(2,1)S(1)} %pad_maximum_fusion.down_ref), custom_call_target="tpu_custom_call" | custom-call | flops 5000000000 | tf_op jit(solution)/shard_map/norm/pallas_call | solution.py:478
  7.3 0.0 copy-done.2
  7.3 0.0 copy-done.3
  7.3 0.0 copy-done.7
  7.4 0.0 copy-done.8
  7.4 0.8 pick.1
  8.1 3.7 %collective-permute-start = (bf16[3,256,128]{2,1,0:T(8,128)(2,1)S(1)}, bf16[3,256,128]{2,1,0:T(8,128)(2,1)S(1)}, u32[]{:S(2)}, u32[]{:S(2)}) collective-permute-start(bf16[3,256,128]{2,1,0:T(8,128)(2,1)S(1)} %get-tuple-element.33), channel_id=1, source_target_pairs={{224,0},{0,32},{32,64},{64,96},{96,128},{128,160},{160,192},{192,2... | collective-permute-start | bytes 589832 | tf_op jit(solution)/shard_map/ppermute | solution.py:385
  11.8 1.3 %collective-permute-start.1 = (bf16[4,256,128]{2,1,0:T(8,128)(2,1)S(1)}, bf16[4,256,128]{2,1,0:T(8,128)(2,1)S(1)}, u32[]{:S(2)}, u32[]{:S(2)}) collective-permute-start(bf16[4,256,128]{2,1,0:T(8,128)(2,1)S(1)} %get-tuple-element.34), channel_id=1, source_target_pairs={{224,0},{0,32},{32,64},{64,96},{96,128},{128,160},{160,192},{192,2... | collective-permute-start | bytes 786440 | tf_op jit(solution)/shard_map/ppermute | solution.py:385
  13.0 0.0 copy-done
  13.0 0.0 copy-done.1
  13.0 0.0 copy-done.6
  13.0 5.9 %own_attention.1 = (f32[3,8,1024]{2,1,0:T(8,128)S(1)}, f32[3,8,128]{2,1,0:T(8,128)S(1)}, f32[8,256]{1,0:T(8,128)S(1)}, f32[8,256]{1,0:T(8,128)S(1)}) custom-call(s32[6]{0:T(128)S(1)} %copy-done.8, bf16[256,6144]{1,0:T(8,128)(2,1)S(1)} %bitcast.8, bf16[256,6144]{1,0:T(8,128)(2,1)S(1)} %bitcast.10, bf16[256,768]{1,0:T(8,128)(2,1)S(1)} %bitcast.14, ...), custom_call_target="tpu_custom_call" | custom-call | flops 1000000000 | tf_op jit(solution)/shard_map/own_attention/pallas_call | solution.py:410
  18.9 0.0 collective-permute-done.kp_ref
  18.9 7.1 %prior_weights.1 = (bf16[3,896,1024]{2,1,0:T(8,128)(2,1)S(1)}, bf16[3,256,128]{2,1,0:T(8,128)(2,1)S(1)}, f32[3,8,128]{2,1,0:T(8,128)S(1)}, f32[8,256]{1,0:T(8,128)S(1)}, f32[8,256]{1,0:T(8,128)S(1)}) custom-call(s32[6]{0:T(128)S(1)} %copy-done.8, bf16[256,6144]{1,0:T(8,128)(2,1)S(1)} %bitcast.9, bf16[256,6144]{1,0:T(8,128)(2,1)S(1)} %bitcast.11, ...), custom_call_target="tpu_custom_call" | custom-call | flops 4000000000 | tf_op jit(solution)/shard_map/prior_weights/pallas_call | solution.py:426
  26.1 4.1 %collective-permute-start.2 = (f32[8,256]{1,0:T(8,128)S(1)}, f32[8,256]{1,0:T(8,128)S(1)}, u32[]{:S(2)}, u32[]{:S(2)}) collective-permute-start(f32[8,256]{1,0:T(8,128)S(1)} %get-tuple-element.43), channel_id=1, source_target_pairs={{32,0},{64,32},{96,64},{128,96},{160,128},{192,160},{224,192},{0,2... | collective-permute-start | bytes 24584 | tf_op jit(solution)/shard_map/ppermute | solution.py:385
  30.1 0.0 collective-permute-done.1.vp_ref
  30.1 5.8 %prior_dscore.1 = (f32[3,8,1024]{2,1,0:T(8,128)S(1)}, f32[3,8,128]{2,1,0:T(8,128)S(1)}, f32[8,256]{1,0:T(8,128)S(1)}) custom-call(s32[6]{0:T(128)S(1)} %copy-done.8, bf16[256,6144]{1,0:T(8,128)(2,1)S(1)} %bitcast.12, bf16[256,768]{1,0:T(8,128)(2,1)S(1)} %bitcast.16, bf16[256,768]{1,0:T(8,128)(2,1)S(1)} %bitcast.19, ...), custom_call_target="tpu_custom_call" | custom-call | flops 4000000000 | tf_op jit(solution)/shard_map/prior_dscore/pallas_call | solution.py:442
  36.0 0.0 copy-start.10
  36.0 0.0 copy-start.4
  36.0 0.0 copy-start.5
  36.0 0.0 collective-permute-done.2.dvh_ref
  36.0 2.0 %gradients.1 = bf16[96,16,128]{2,1,0:T(8,128)(2,1)S(1)} custom-call(s32[6]{0:T(128)S(1)} %copy-done.8, bf16[256,8192]{1,0:T(8,128)(2,1)S(1)} %get-tuple-element.29.normed_ref, f32[8,256]{1,0:T(8,128)S(1)} %get-tuple-element.41.dqm_ref, f32[8,256]{1,0:T(8,128)S(1)} %get-tuple-element.42.dvm_ref, f32[8,256]{1,0:T(8,128)S(1)} %collective-permute-done.2.dvh_ref, ...), custom_call_target="tpu_custom_call" | custom-call | tf_op jit(solution)/shard_map/gradients/pallas_call | solution.py:516
  38.0 15.3 %all_to_all.15 = bf16[32,3,16,128]{3,2,1,0:T(8,128)(2,1)S(1)} all-to-all(bf16[32,3,16,128]{3,2,1,0:T(8,128)(2,1)S(1)} %bitcast.20), channel_id=1, replica_groups={{0,1,2,3,32,33,34,35,64,65,66,67,96,97,98,99,128,129,130,131,160,161,16..., dimensions={0} | all-to-all | bytes 786432 | tf_op jit(solution)/shard_map/all_to_all | solution.py:372
  53.3 0.1 reduce_sum.24
  53.4 15.4 %all_to_all.16 = bf16[8,3,16,128]{3,2,1,0:T(8,128)(2,1)S(1)} all-to-all(bf16[8,3,16,128]{3,2,1,0:T(8,128)(2,1)S(1)} %broadcast_in_dim.7), channel_id=1, replica_groups={{0,4,8,12,16,20,24,28},{1,5,9,13,17,21,25,29},{2,6,10,14,18,22,26,30},{..., dimensions={0} | all-to-all | bytes 196608 | tf_op jit(solution)/shard_map/all_to_all | solution.py:372
  68.9 0.8 broadcast_in_dim.8
  69.7 5.5 %all-to-all-start.2 = ((bf16[32,3,16,128]{3,2,1,0:T(8,128)(2,1)}), bf16[32,3,16,128]{3,2,1,0:T(8,128)(2,1)S(1)}, u32[]{:S(2)}, u32[]{:S(2)}) async-start(bf16[32,3,16,128]{3,2,1,0:T(8,128)(2,1)} %broadcast_in_dim.8), calls=%async_computation.2 | async-start | bytes 786432 | tf_op jit(solution)/shard_map/all_to_all | solution.py:372
  75.2 0.0 copy-done.10
  75.3 10.2 %all-to-all-done.2 = bf16[32,3,16,128]{3,2,1,0:T(8,128)(2,1)S(1)} async-done(((bf16[32,3,16,128]{3,2,1,0:T(8,128)(2,1)}), bf16[32,3,16,128]{3,2,1,0:T(8,128)(2,1)S(1)}, u32[]{:S(2)}, u32[]{:S(2)}) %all-to-all-start.2) | async-done | bytes 393248 | tf_op jit(solution)/shard_map/all_to_all | solution.py:372
  85.5 0.0 copy-done.4
  85.5 0.0 copy-done.5
  85.5 1.2 %clip.1 = (f32[8,8192]{1,0:T(8,128)}, f32[8,6144]{1,0:T(8,128)}, f32[8,8192]{1,0:T(8,128)}, f32[8,768]{1,0:T(8,128)}, f32[1,8192]{1,0:T(1,128)}) custom-call(bf16[96,16,128]{2,1,0:T(8,128)(2,1)S(1)} %bitcast.21, bf16[8,8192]{1,0:T(8,128)(2,1)S(1)} %copy-done.5, bf16[8,8192]{1,0:T(8,128)(2,1)S(1)} %copy-done.4, bf16[1,8192]{1,0:T(2,128)(2,1)S(1)} %reshape.27.scale_ref), custom_call_target="tpu_custom_call" | custom-call | tf_op jit(solution)/shard_map/clip/pallas_call | solution.py:535
  (3 shorter events, 0.1 us)
Async XLA Ops:
  2.4 2.2 %copy-start.9 = (bf16[1,256,8192]{2,1,0:T(8,128)(2,1)S(1)}, bf16[1,256,8192]{2,1,0:T(8,128)(2,1)}, u32[]{:S(2)}) copy-start(bf16[1,256,8192]{2,1,0:T(8,128)(2,1)} %param.11) | copy-start | bytes 12582916
  4.6 2.8 %copy-start.2 = (bf16[1,256,768]{2,1,0:T(8,128)(2,1)S(1)}, bf16[1,256,768]{2,1,0:T(8,128)(2,1)}, u32[]{:S(2)}) copy-start(bf16[1,256,768]{2,1,0:T(8,128)(2,1)} %param.13) | copy-start | bytes 1179652
  4.6 2.8 %copy-start.3 = (bf16[1,256,768]{2,1,0:T(8,128)(2,1)S(1)}, bf16[1,256,768]{2,1,0:T(8,128)(2,1)}, u32[]{:S(2)}) copy-start(bf16[1,256,768]{2,1,0:T(8,128)(2,1)} %param.14) | copy-start | bytes 1179652
  4.6 2.8 %copy-start.7 = (bf16[8,768]{1,0:T(8,128)(2,1)S(1)}, bf16[8,768]{1,0:T(8,128)(2,1)}, u32[]{:S(2)}) copy-start(bf16[8,768]{1,0:T(8,128)(2,1)} %vup_ref.7) | copy-start | bytes 36868
  4.6 2.8 %copy-start.8 = (s32[6]{0:T(128)S(1)}, s32[6]{0:T(128)}, u32[]{:S(2)}) copy-start(s32[6]{0:T(128)} %ids_ref.9) | copy-start | bytes 76
  4.6 8.5 %copy-start = (bf16[1,256,6144]{2,1,0:T(8,128)(2,1)S(1)}, bf16[1,256,6144]{2,1,0:T(8,128)(2,1)}, u32[]{:S(2)}) copy-start(bf16[1,256,6144]{2,1,0:T(8,128)(2,1)} %param.12) | copy-start | bytes 9437188
  4.6 8.4 %copy-start.1 = (bf16[1,256,6144]{2,1,0:T(8,128)(2,1)S(1)}, bf16[1,256,6144]{2,1,0:T(8,128)(2,1)}, u32[]{:S(2)}) copy-start(bf16[1,256,6144]{2,1,0:T(8,128)(2,1)} %param.15) | copy-start | bytes 9437188
  4.6 8.4 %copy-start.6 = (bf16[8,6144]{1,0:T(8,128)(2,1)S(1)}, bf16[8,6144]{1,0:T(8,128)(2,1)}, u32[]{:S(2)}) copy-start(bf16[8,6144]{1,0:T(8,128)(2,1)} %qup_ref.5) | copy-start | bytes 294916
  8.1 10.8 %collective-permute-start = (bf16[3,256,128]{2,1,0:T(8,128)(2,1)S(1)}, bf16[3,256,128]{2,1,0:T(8,128)(2,1)S(1)}, u32[]{:S(2)}, u32[]{:S(2)}) collective-permute-start(bf16[3,256,128]{2,1,0:T(8,128)(2,1)S(1)} %get-tuple-element.33), channel_id=1, source_target_pairs={{224,0},{0,32},{32,64},{64,96},{96,128},{128,160},{160,192},{192,2... | collective-permute-start | bytes 589832 | tf_op jit(solution)/shard_map/ppermute | solution.py:385
  11.8 18.4 %collective-permute-start.1 = (bf16[4,256,128]{2,1,0:T(8,128)(2,1)S(1)}, bf16[4,256,128]{2,1,0:T(8,128)(2,1)S(1)}, u32[]{:S(2)}, u32[]{:S(2)}) collective-permute-start(bf16[4,256,128]{2,1,0:T(8,128)(2,1)S(1)} %get-tuple-element.34), channel_id=1, source_target_pairs={{224,0},{0,32},{32,64},{64,96},{96,128},{128,160},{160,192},{192,2... | collective-permute-start | bytes 786440 | tf_op jit(solution)/shard_map/ppermute | solution.py:385
  26.1 9.9 %collective-permute-start.2 = (f32[8,256]{1,0:T(8,128)S(1)}, f32[8,256]{1,0:T(8,128)S(1)}, u32[]{:S(2)}, u32[]{:S(2)}) collective-permute-start(f32[8,256]{1,0:T(8,128)S(1)} %get-tuple-element.43), channel_id=1, source_target_pairs={{32,0},{64,32},{96,64},{128,96},{160,128},{192,160},{224,192},{0,2... | collective-permute-start | bytes 24584 | tf_op jit(solution)/shard_map/ppermute | solution.py:385
  36.0 39.2 %copy-start.10 = (bf16[8192]{0:T(1024)(128)(2,1)S(1)}, bf16[8192]{0:T(1024)(128)(2,1)}, u32[]{:S(2)}) copy-start(bf16[8192]{0:T(1024)(128)(2,1)} %param.16) | copy-start | bytes 49156
  36.0 49.5 %copy-start.4 = (bf16[8,8192]{1,0:T(8,128)(2,1)S(1)}, bf16[8,8192]{1,0:T(8,128)(2,1)}, u32[]{:S(2)}) copy-start(bf16[8,8192]{1,0:T(8,128)(2,1)} %vd_ref.1) | copy-start | bytes 393220
  36.0 49.5 %copy-start.5 = (bf16[8,8192]{1,0:T(8,128)(2,1)S(1)}, bf16[8,8192]{1,0:T(8,128)(2,1)}, u32[]{:S(2)}) copy-start(bf16[8,8192]{1,0:T(8,128)(2,1)} %qd_ref.1) | copy-start | bytes 393220
  69.7 15.8 %all-to-all-start.2 = ((bf16[32,3,16,128]{3,2,1,0:T(8,128)(2,1)}), bf16[32,3,16,128]{3,2,1,0:T(8,128)(2,1)S(1)}, u32[]{:S(2)}, u32[]{:S(2)}) async-start(bf16[32,3,16,128]{3,2,1,0:T(8,128)(2,1)} %broadcast_in_dim.8), calls=%async_computation.2 | async-start | bytes 786432 | tf_op jit(solution)/shard_map/all_to_all | solution.py:372

commit v3 on v2

--- a/solution.py
+++ b/solution.py
@@ -21,6 +21,7 @@
 LOG2_E = 1.4426950408889634
 TILES = 96
 QB_TILE = 64
+PART = TILES // 2
 F32 = jnp.float32
 BF16 = jnp.bfloat16
 BOTH = ("seq", "dp")
@@ -84,18 +85,22 @@
     return slice(c * HALF, (c + 1) * HALF)
 
 
-def stacked(ref, i, c):
+def share(part):
+    return range(part * WIDE, (part + 1) * WIDE)
+
+
+def stacked(ref, i, c, part):
     return jnp.concatenate(
-        [ref[i, token_rows(c), j * HEAD_SIZE : (j + 1) * HEAD_SIZE] for j in range(SHARE)], axis=0
+        [ref[i, token_rows(c), j * HEAD_SIZE : (j + 1) * HEAD_SIZE] for j in share(part)], axis=0
     )
 
 
-def stacked_grads(ref, ids_ref, place, c):
+def stacked_grads(ref, ids_ref, place, c, part):
     start = head_at(ids_ref, place) * LANES
     return jnp.concatenate(
         [
             ref[token_rows(c), pl.ds(pl.multiple_of(start + j * HEAD_SIZE, HEAD_SIZE), HEAD_SIZE)]
-            for j in range(SHARE)
+            for j in share(part)
         ],
         axis=0,
     )
@@ -104,7 +109,7 @@
 def causal_mask():
     key_id = lax.broadcasted_iota(jnp.int32, (HALF, HALF), 0)
     query_id = lax.broadcasted_iota(jnp.int32, (HALF, HALF), 1)
-    return jnp.concatenate([key_id <= query_id] * SHARE, axis=1)
+    return jnp.concatenate([key_id <= query_id] * WIDE, axis=1)
 
 
 def transposed(array):
@@ -134,20 +139,27 @@
     return functools.reduce(jnp.add, [jnp.sum(p, axis=0, keepdims=True) for p in parts])
 
 
-def keep_dq(dq_scr, i, c, dq_t):
+def keep_dq(dq_scr, i, c, part, dq_t):
     dq_b = (dq_t * FACTOR).astype(BF16)
-    for j in range(SHARE):
-        dq_scr[i, j * HEAD_SIZE : (j + 1) * HEAD_SIZE, token_rows(c)] = dq_b[:, j * HALF : (j + 1) * HALF]
-
-
-UNITS = [(i, c) for i in range(3) for c in range(2)]
+    for n, j in enumerate(share(part)):
+        dq_scr[i, j * HEAD_SIZE : (j + 1) * HEAD_SIZE, token_rows(c)] = dq_b[:, n * HALF : (n + 1) * HALF]
+
+
+def accumulate(totals, name, first, value):
+    totals[name] = value if first else totals[name] + value
+
+
+WIDE = 2
+AHEAD = 4
+UNITS = [(i, c, part) for i in range(3) for c in range(2) for part in range(SHARE // WIDE)]
 
 
 def pipelined(before, after):
-    ahead = before(*UNITS[0])
+    states = [before(*unit) for unit in UNITS[:AHEAD]]
     for n, unit in enumerate(UNITS):
-        state, ahead = ahead, before(*UNITS[n + 1]) if n + 1 < len(UNITS) else None
-        after(*unit, state)
+        if n + AHEAD < len(UNITS):
+            states.append(before(*UNITS[n + AHEAD]))
+        after(*unit, states.pop(0))
 
 
 def own_kernel(
@@ -158,18 +170,18 @@
     heads = {}
     totals = {}
 
-    def before(i, c):
-        if c == 0:
+    def before(i, c, part):
+        if c == 0 and part == 0:
             small = head_cols(ids_ref, 3 + i, HEAD_SIZE)
             keys = k_ref[:, small]
             vup, qup = vup_ref[:, small], qup_ref[:, head_cols(ids_ref, 3 + i, LANES)]
             q_scr[i] = adapted(q_ref[:, head_cols(ids_ref, 3 + i, LANES)], qm_ref[...], qup)
             heads[i] = (keys, transposed(keys), adapted(v_ref[:, small], vm_ref[...], vup), qup, vup)
         keys, _, values, _, _ = heads[i]
-        grads = stacked_grads(g_ref, ids_ref, 3 + i, c)
-        return own_scores(keys, stacked(q_scr, i, c), c, mask), nt(values[: (c + 1) * HALF], grads), grads
-
-    def after(i, c, state):
+        grads = stacked_grads(g_ref, ids_ref, 3 + i, c, part)
+        return own_scores(keys, stacked(q_scr, i, c, part), c, mask), nt(values[: (c + 1) * HALF], grads), grads
+
+    def after(i, c, part, state):
         parts, dprob, grads = state
         _, keys_t, _, qup, vup = heads[i]
         probs = softmax(parts)
@@ -178,12 +190,15 @@
         delta = summed_over_keys([w.astype(F32) * d for w, d in zip(weights, dprobs)])
         dscore = [(p * (d - delta)).astype(BF16) for p, d in zip(probs, dprobs)]
         near = (c + 1) * HALF
-        keep_dq(dq_scr, i, c, nn(keys_t[:, :near], jnp.concatenate(dscore, axis=0)))
+        keep_dq(dq_scr, i, c, part, nn(keys_t[:, :near], jnp.concatenate(dscore, axis=0)))
         term = nn(jnp.concatenate(weights, axis=0), grads)
+        accumulate(totals, "low", c == 0 and part == 0, term[:HALF])
         if c == 0:
-            totals["low"] = term
             return
-        dv = jnp.concatenate([totals["low"] + term[:HALF], term[HALF:]], axis=0).astype(BF16)
+        accumulate(totals, "high", part == 0, term[HALF:])
+        if part < SHARE // WIDE - 1:
+            return
+        dv = jnp.concatenate([totals["low"], totals["high"]], axis=0).astype(BF16)
         dq_t = dq_scr[i]
         qb_ref[i] = 2.0 * nt(qmt_ref[...], dq_t)
         vb_ref[i] = 2.0 * nn(vmt_ref[...], dv)
@@ -204,30 +219,34 @@
     heads = {}
     totals = {"dv": dvm1_ref[...]}
 
-    def before(i, c):
-        if c == 0:
+    def before(i, c, part):
+        if c == 0 and part == 0:
             small = head_cols(ids_ref, i, HEAD_SIZE)
             qup = qup_ref[:, head_cols(ids_ref, i, LANES)]
             q_scr[i] = adapted(q_ref[:, head_cols(ids_ref, i, LANES)], qm_ref[...], qup)
             heads[i] = (k_ref[:, small], kp_ref[i], vup_ref[:, small])
         keys, prior, _ = heads[i]
-        queries = stacked(q_scr, i, c)
+        queries = stacked(q_scr, i, c, part)
         return own_scores(keys, queries, c, mask), nt(prior, queries) * (FACTOR * LOG2_E)
 
-    def after(i, c, state):
+    def after(i, c, part, state):
         own, prior = state
         probs = softmax(own + [prior])
         weights = jnp.concatenate([p.astype(BF16) for p in probs], axis=0)
         rows = 3 * HALF + c * HALF
-        w_ref[i, c * 3 * HALF : c * 3 * HALF + rows] = weights
-        grads = stacked_grads(g_ref, ids_ref, i, c)
+        w_ref[i, c * 3 * HALF : c * 3 * HALF + rows, part * WIDE * HALF : (part + 1) * WIDE * HALF] = weights
+        grads = stacked_grads(g_ref, ids_ref, i, c, part)
         term = nn(weights, grads)
+        near = (c + 1) * HALF
+        accumulate(totals, "low", c == 0 and part == 0, term[:HALF])
+        accumulate(totals, "prior", c == 0 and part == 0, term[near:])
         if c == 0:
-            totals["low"] = term
             return
-        low = totals["low"]
-        dv = jnp.concatenate([low[:HALF] + term[:HALF], term[HALF : 2 * HALF]], axis=0).astype(BF16)
-        dv_prior = (low[HALF:] + term[2 * HALF :]).astype(BF16)
+        accumulate(totals, "high", part == 0, term[HALF:near])
+        if part < SHARE // WIDE - 1:
+            return
+        dv = jnp.concatenate([totals["low"], totals["high"]], axis=0).astype(BF16)
+        dv_prior = totals["prior"].astype(BF16)
         _, _, vup = heads[i]
         dvp_ref[i] = dv_prior
         vb_ref[i] = 2.0 * nn(vmt_ref[...], dv)
@@ -250,8 +269,8 @@
     heads = {}
     totals = {"dq": dqm1_ref[...]}
 
-    def before(i, c):
-        if c == 0:
+    def before(i, c, part):
+        if c == 0 and part == 0:
             small = head_cols(ids_ref, i, HEAD_SIZE)
             vup = vup_ref[:, small]
             heads[i] = (
@@ -261,21 +280,22 @@
                 vp_ref[i],
             )
         _, _, values, prior = heads[i]
-        grads = stacked_grads(g_ref, ids_ref, i, c)
+        grads = stacked_grads(g_ref, ids_ref, i, c, part)
         return nt(values[: (c + 1) * HALF], grads), nt(prior, grads)
 
-    def after(i, c, dprobs):
+    def after(i, c, part, dprobs):
         keys_t, prior_t, _, _ = heads[i]
         near = (c + 1) * HALF
         start = c * 3 * HALF
+        cols = slice(part * WIDE * HALF, (part + 1) * WIDE * HALF)
         weights = [
-            w_ref[i, start : start + near].astype(F32),
-            w_ref[i, start + near : start + near + TOKENS].astype(F32),
+            w_ref[i, start : start + near, cols].astype(F32),
+            w_ref[i, start + near : start + near + TOKENS, cols].astype(F32),
         ]
         delta = summed_over_keys([w * d for w, d in zip(weights, dprobs)])
         dscore = [(w * (d - delta)).astype(BF16) for w, d in zip(weights, dprobs)]
-        keep_dq(dq_scr, i, c, nn(keys_t[:, :near], dscore[0]) + nn(prior_t, dscore[1]))
-        if c == 0:
+        keep_dq(dq_scr, i, c, part, nn(keys_t[:, :near], dscore[0]) + nn(prior_t, dscore[1]))
+        if c == 0 or part < SHARE // WIDE - 1:
             return
         dq_t = dq_scr[i]
         qb_ref[i] = 2.0 * nt(qmt_ref[...], dq_t)
@@ -287,70 +307,70 @@
 
 
 def gather_kernel(
-    ids_ref, normed_ref, dqm_ref, dvm_ref, dvh_ref,
-    qb1_ref, vb1_ref, qb2_ref, vb2_ref, out_ref, buf,
+    ids_ref, normed_ref, dqm_ref, dvm_ref, dvh_ref, qb1_ref, vb1_ref, qb2_ref, vb2_ref,
+    keep_ref, send_ref, tiles, buf,
 ):
-    step = pl.program_id(0)
-
-    @pl.when(step < 4)
-    def _():
-        dq = dqm_ref[...]
-        dv = dvm_ref[...] + dvh_ref[...]
-        mids = jnp.concatenate([dq, dv], axis=0).astype(BF16)
-        for j in range(4):
-            part = nn(mids, normed_ref[:, j * 512 : (j + 1) * 512]).astype(BF16)
-            for k in range(4):
-                out_ref[4 * j + k] = part[:, k * HEAD_SIZE : (k + 1) * HEAD_SIZE]
-
-    @pl.when(step == 4)
-    def _():
-        buf[27:32] = jnp.zeros((5, 16, HEAD_SIZE), F32)
-        for i in range(3):
-            for base, qb_ref, vb_ref in ((0, qb2_ref, vb2_ref), (3, qb1_ref, vb1_ref)):
-                head = head_at(ids_ref, base + i)
-                upper = head >= 3
-                row = pl.multiple_of(jnp.where(upper, 8, 0), 8)
-                place = jnp.where(upper, head - 3, head)
-                for k in range(SHARE):
-                    buf[place * SHARE + k, pl.ds(row, 8), :] = qb_ref[i][:, k * HEAD_SIZE : (k + 1) * HEAD_SIZE]
-                buf[24 + place, pl.ds(row, 8), :] = vb_ref[i]
-        for t in range(16):
-            out_ref[t] = buf[t].astype(BF16)
-
-    @pl.when(step == 5)
-    def _():
-        for t in range(16):
-            out_ref[t] = buf[16 + t].astype(BF16)
-
-
-def clip_kernel(limit, sum_ref, qd_ref, vd_ref, scale_ref, qa_ref, qb_ref, va_ref, vb_ref, gain_ref, gains):
+    mids = jnp.concatenate([dqm_ref[...], dvm_ref[...] + dvh_ref[...]], axis=0).astype(BF16)
+    buf[27:32] = jnp.zeros((5, 16, HEAD_SIZE), F32)
+    for i in range(3):
+        for base, qb_ref, vb_ref in ((0, qb2_ref, vb2_ref), (3, qb1_ref, vb1_ref)):
+            head = head_at(ids_ref, base + i)
+            upper = head >= 3
+            row = pl.multiple_of(jnp.where(upper, 8, 0), 8)
+            place = jnp.where(upper, head - 3, head)
+            for k in range(SHARE):
+                buf[place * SHARE + k, pl.ds(row, 8), :] = qb_ref[i][:, k * HEAD_SIZE : (k + 1) * HEAD_SIZE]
+            buf[24 + place, pl.ds(row, 8), :] = vb_ref[i]
+    for j in range(16):
+        part = nn(mids, normed_ref[:, j * 512 : (j + 1) * 512]).astype(BF16)
+        for k in range(4):
+            t = 4 * j + k
+            tiles[t // PART, t % PART] = part[:, k * HEAD_SIZE : (k + 1) * HEAD_SIZE]
+    for t in range(QB_TILE, TILES):
+        tiles[t // PART, t % PART] = buf[t - QB_TILE].astype(BF16)
+    core = lax.axis_index("dp") % 2
+    keep_ref[...] = tiles[core]
+    send_ref[...] = tiles[1 - core]
+
+
+def clip_kernel(
+    limit, mine_ref, other_ref, qd_ref, vd_ref, scale_ref,
+    qa_ref, qb_ref, va_ref, vb_ref, gain_ref, gains, both,
+):
+    core = lax.axis_index("dp") % 2
+    both[core] = mine_ref[...]
+    both[1 - core] = other_ref[...]
+
+    def summed(t):
+        return both[t // PART, t % PART].astype(F32)
+
     total = jnp.zeros((16, HEAD_SIZE), F32)
     gain_total = jnp.zeros((1, HEAD_SIZE), F32)
     for t in range(QB_TILE):
         cols = slice(t * HEAD_SIZE, (t + 1) * HEAD_SIZE)
-        tile = sum_ref[t].astype(F32)
+        tile = summed(t)
         total = total + tile * tile
         mixed = qd_ref[:, cols].astype(F32) * tile[:RANK] + vd_ref[:, cols].astype(F32) * tile[RANK:]
         gain = jnp.sum(mixed, axis=0, keepdims=True) / scale_ref[:, cols].astype(F32)
         gains[:, cols] = gain
         gain_total = gain_total + gain * gain
     for t in range(QB_TILE, QB_TILE + 27):
-        tile = sum_ref[t].astype(F32)
+        tile = summed(t)
         total = total + tile * tile
     squares = jnp.sum(total, keepdims=True) + jnp.sum(gain_total, keepdims=True)
     factor = jnp.minimum(1.0, limit / jnp.sqrt(squares))
     gain_ref[...] = gains[...] * factor
     for t in range(QB_TILE):
         cols = slice(t * HEAD_SIZE, (t + 1) * HEAD_SIZE)
-        tile = sum_ref[t].astype(F32) * factor
+        tile = summed(t) * factor
         qa_ref[:, cols] = tile[:RANK]
         va_ref[:, cols] = tile[RANK:]
     for t in range(24):
-        tile = sum_ref[QB_TILE + t].astype(F32) * factor
+        tile = summed(QB_TILE + t) * factor
         qb_ref[:, t * HEAD_SIZE : (t + 1) * HEAD_SIZE] = tile[:RANK]
         qb_ref[:, (24 + t) * HEAD_SIZE : (25 + t) * HEAD_SIZE] = tile[RANK:]
     for t in range(3):
-        tile = sum_ref[QB_TILE + 24 + t].astype(F32) * factor
+        tile = summed(QB_TILE + 24 + t) * factor
         vb_ref[:, t * HEAD_SIZE : (t + 1) * HEAD_SIZE] = tile[:RANK]
         vb_ref[:, (3 + t) * HEAD_SIZE : (4 + t) * HEAD_SIZE] = tile[RANK:]
 
@@ -364,7 +384,7 @@
     return list(found.values())
 
 
-PLANE = groups_along(("y", "xh", "xl", "core"))
+PLANE = groups_along(("y", "xh", "xl"))
 COLUMN = groups_along(("z",))
 
 
@@ -372,13 +392,19 @@
     return lax.all_to_all(array, BOTH, 0, 0, tiled=True, axis_index_groups=groups)
 
 
-def sum_over_devices(tiles):
-    shares = tiles.reshape(32, 3, 16, HEAD_SIZE)
+def other_core(array):
+    return lax.ppermute(array, "dp", [(i, i ^ 1) for i in range(32)])
+
+
+def sum_over_devices(keep, send):
+    shares = (keep.astype(F32) + other_core(send).astype(F32)).astype(BF16)
+    shares = shares.reshape(16, 3, 16, HEAD_SIZE)
     mine = jnp.sum(exchange(shares, PLANE).astype(F32), axis=0).astype(BF16)
     copies = jnp.broadcast_to(mine[None], (8, 3, 16, HEAD_SIZE))
     mine = jnp.sum(exchange(copies, COLUMN).astype(F32), axis=0).astype(BF16)
-    copies = jnp.broadcast_to(mine[None], (32, 3, 16, HEAD_SIZE))
-    return exchange(copies, PLANE).reshape(TILES, 16, HEAD_SIZE)
+    copies = jnp.broadcast_to(mine[None], (16, 3, 16, HEAD_SIZE))
+    whole_part = exchange(copies, PLANE).reshape(PART, 16, HEAD_SIZE)
+    return whole_part, other_core(whole_part)
 
 
 def from_behind(block, distance):
@@ -513,23 +539,19 @@
         ids, g, k, v, vm, qmt, qup, vup, keys_prior, values_prior, w, dvp, vbp, dqm1
     )
 
-    tiles = pl.pallas_call(
+    keep, send = pl.pallas_call(
         gather_kernel,
-        out_shape=jax.ShapeDtypeStruct((TILES, 16, HEAD_SIZE), BF16),
-        grid_spec=pltpu.PrefetchScalarGridSpec(
-            num_scalar_prefetch=1,
-            grid=(6,),
-            in_specs=[pl.BlockSpec((TOKENS, 2048), lambda i, ids: (0, jnp.minimum(i, 3)))]
-            + [whole((RANK, TOKENS))] * 3
-            + [whole((3, RANK, LANES)), whole((3, RANK, HEAD_SIZE))] * 2,
-            out_specs=pl.BlockSpec((16, 16, HEAD_SIZE), lambda i, ids: (i, 0, 0)),
-            scratch_shapes=[pltpu.VMEM((32, 16, HEAD_SIZE), F32)],
-        ),
+        out_shape=[struct((PART, 16, HEAD_SIZE), BF16)] * 2,
+        in_specs=[SMEM] + [VMEM] * 8,
+        out_specs=[VMEM] * 2,
+        scratch_shapes=[
+            pltpu.VMEM((2, PART, 16, HEAD_SIZE), BF16), pltpu.VMEM((32, 16, HEAD_SIZE), F32),
+        ],
         compiler_params=params(16),
         name="gradients",
     )(ids, normed, dqm, dvm, handed, qb1, vb1, qb2, vb2)
 
-    summed = sum_over_devices(tiles)
+    mine, other = sum_over_devices(keep, send)
 
     listed_items = RANK * (2 * WIDTH + KV_HEADS * LANES + KV_HEADS * HEAD_SIZE) + WIDTH
     qa, qb, va, vb, gain = pl.pallas_call(
@@ -541,10 +563,10 @@
             jax.ShapeDtypeStruct((RANK, KV_HEADS * HEAD_SIZE), F32),
             jax.ShapeDtypeStruct((1, WIDTH), F32),
         ],
-        scratch_shapes=[pltpu.VMEM((1, WIDTH), F32)],
+        scratch_shapes=[pltpu.VMEM((1, WIDTH), F32), pltpu.VMEM((2, PART, 16, HEAD_SIZE), BF16)],
         compiler_params=params(16),
         name="clip",
-    )(summed, query_down_weight, value_down_weight, scale)
+    )(mine, other, query_down_weight, value_down_weight, scale)
     return (qa, qb, va, vb, gain.reshape(WIDTH))
 
 

time: 87.1 us -> 82.1 us (0.943)
  waiting for transfers between devices: 10.3 us -> 2.12 us
  blocking collectives: 30.8 us -> 36.1 us
  Pallas kernels: 25.5 us -> 23.3 us
    all_to_all x1 -> x0, waiting for transfers between devices: 10.2 us -> none  [exchange(): lax.all_to_all(array, BOTH, 0, 0, tiled=True, axis_index_groups=groups)]
    ppermute x0 -> x2, starting transfers between devices: none -> 6.29 us  [other_core(): return lax.ppermute(array, 'dp', [(i, i ^ 1) for i in range(32)])]
    all_to_all x1 -> x0, starting transfers between devices: 5.52 us -> none  [exchange(): lax.all_to_all(array, BOTH, 0, 0, tiled=True, axis_index_groups=groups)]
    all_to_all x2 -> x3, blocking collectives: 30.8 us -> 36.1 us  [exchange(): lax.all_to_all(array, BOTH, 0, 0, tiled=True, axis_index_groups=groups)]
    ppermute x0 -> x2, waiting for transfers between devices: none -> 2.12 us  [other_core(): return lax.ppermute(array, 'dp', [(i, i ^ 1) for i in range(32)])]
  transfers between devices with their start and end apart: 4 -> 5, of which waited for: 1 -> 2; matrix products, arithmetic and copies ran while one was open for 0% -> 0% of each run, Pallas kernels for 22% -> 21%
where the time goes in v3:
time: 82.1 us; the launch traced here: 81.8 us
  blocking collectives  36.1 us (44%)
  Pallas kernels  23.3 us (28%)
  starting transfers between devices  15.3 us (19%)
  local copies, waits for them, and re-layouts  3.04 us (4%)
  waiting for transfers between devices  2.12 us (3%)
  other arithmetic  1.12 us (1%)
    all_to_all x3, blocking collectives, exchange(): lax.all_to_all(array, BOTH, 0, 0, tiled=True, axis_index_groups=groups)  36.1 us
    ppermute x3, starting transfers between devices, from_behind(): lax.ppermute(block, 'seq', [((i - distance) % 8, i) for i in range(8)])  8.99 us
    pallas_call x1, Pallas kernels, weights_call(): pl.pallas_call(weights_kernel, out_shape=[struct((3, 7 * HALF, LANES), BF...  6.41 us
    ppermute x2, starting transfers between devices, other_core(): return lax.ppermute(array, 'dp', [(i, i ^ 1) for i in range(32)])  6.29 us
    pallas_call x1, Pallas kernels, own_call(): pl.pallas_call(own_kernel, out_shape=[struct((3, RANK, LANES), F32), stru...  5.69 us
    pallas_call x1, Pallas kernels, dscore_call(): pl.pallas_call(dscore_kernel, out_shape=[struct((3, RANK, LANES), F32), s...  5.31 us
    pallas_call x1, Pallas kernels, shards(): pl.pallas_call(norm_kernel, out_shape=[struct((TOKENS, WIDTH), BF16), str...  2.7 us
    unnamed x22, local copies, waits for them, and re-layouts  2.24 us
  transfers between devices with their start and end apart: 5, of which 2 were waited for; matrix products, arithmetic and copies ran while one was open for 0% of the time, Pallas kernels for 21%

profile of v3, /device:TPU:1, one launch (start us, length us, event | category | flops | bytes accessed | tf_op | source)
XLA Modules:
  0.0 81.8 jit_solution(17400256042054276474)
XLA Ops:
  0.6 0.7 broadcast_in_dim.6
  1.4 1.0 %pad_maximum_fusion.down_ref = bf16[32,8192]{1,0:T(8,128)(2,1)S(1)} fusion(bf16[16,8192]{1,0:T(8,128)(2,1)S(1)} %broadcast_in_dim.6, bf16[8,8192]{1,0:T(8,128)(2,1)} %vd_ref.1, bf16[8,8192]{1,0:T(8,128)(2,1)} %qd_ref.1), kind=kLoop, calls=%fused_computation | loop fusion | flops 1572864 | bytes 1048576 | tf_op jit(solution)/shard_map/concatenate | solution.py:500
  2.4 0.0 copy-start.9
  2.4 2.2 %copy-done.9 = bf16[1,256,8192]{2,1,0:T(8,128)(2,1)S(1)} copy-done((bf16[1,256,8192]{2,1,0:T(8,128)(2,1)S(1)}, bf16[1,256,8192]{2,1,0:T(8,128)(2,1)}, u32[]{:S(2)}) %copy-start.9) | copy-done | bytes 4194328
  4.6 0.0 copy-start.2
  4.6 0.0 copy-start.3
  4.6 0.0 copy-start.7
  4.6 0.0 copy-start.8
  4.6 0.0 copy-start
  4.6 0.0 copy-start.1
  4.6 0.0 copy-start.6
  4.6 2.7 %norm.1 = (bf16[256,8192]{1,0:T(8,128)(2,1)S(1)}, bf16[256,8]{1,0:T(8,128)(2,1)S(1)}, bf16[256,8]{1,0:T(8,128)(2,1)S(1)}, bf16[8,256]{1,0:T(8,128)(2,1)S(1)}, bf16[8,256]{1,0:T(8,128)(2,1)S(1)}) custom-call(bf16[256,8192]{1,0:T(8,128)(2,1)S(1)} %bitcast.22, bf16[32,8192]{1,0:T(8,128)(2,1)S(1)} %pad_maximum_fusion.down_ref), custom_call_target="tpu_custom_call" | custom-call | flops 5000000000 | tf_op jit(solution)/shard_map/norm/pallas_call | solution.py:504
  7.3 0.0 copy-done.2
  7.3 0.0 copy-done.3
  7.3 0.0 copy-done.7
  7.4 0.0 copy-done.8
  7.4 0.8 pick.1
  8.1 3.7 %collective-permute-start = (bf16[3,256,128]{2,1,0:T(8,128)(2,1)S(1)}, bf16[3,256,128]{2,1,0:T(8,128)(2,1)S(1)}, u32[]{:S(2)}, u32[]{:S(2)}) collective-permute-start(bf16[3,256,128]{2,1,0:T(8,128)(2,1)S(1)} %get-tuple-element.35), channel_id=1, source_target_pairs={{224,0},{0,32},{32,64},{64,96},{96,128},{128,160},{160,192},{192,2... | collective-permute-start | bytes 589832 | tf_op jit(solution)/shard_map/ppermute | solution.py:411
  11.8 1.3 %collective-permute-start.1 = (bf16[4,256,128]{2,1,0:T(8,128)(2,1)S(1)}, bf16[4,256,128]{2,1,0:T(8,128)(2,1)S(1)}, u32[]{:S(2)}, u32[]{:S(2)}) collective-permute-start(bf16[4,256,128]{2,1,0:T(8,128)(2,1)S(1)} %get-tuple-element.36), channel_id=1, source_target_pairs={{224,0},{0,32},{32,64},{64,96},{96,128},{128,160},{160,192},{192,2... | collective-permute-start | bytes 786440 | tf_op jit(solution)/shard_map/ppermute | solution.py:411
  13.0 0.0 copy-done
  13.0 0.0 copy-done.1
  13.0 0.0 copy-done.6
  13.0 5.7 %own_attention.1 = (f32[3,8,1024]{2,1,0:T(8,128)S(1)}, f32[3,8,128]{2,1,0:T(8,128)S(1)}, f32[8,256]{1,0:T(8,128)S(1)}, f32[8,256]{1,0:T(8,128)S(1)}) custom-call(s32[6]{0:T(128)S(1)} %copy-done.8, bf16[256,6144]{1,0:T(8,128)(2,1)S(1)} %bitcast.8, bf16[256,6144]{1,0:T(8,128)(2,1)S(1)} %bitcast.10, bf16[256,768]{1,0:T(8,128)(2,1)S(1)} %bitcast.14, ...), custom_call_target="tpu_custom_call" | custom-call | flops 1000000000 | tf_op jit(solution)/shard_map/own_attention/pallas_call | solution.py:436
  18.7 0.0 collective-permute-done.kp_ref
  18.7 6.4 %prior_weights.1 = (bf16[3,896,1024]{2,1,0:T(8,128)(2,1)S(1)}, bf16[3,256,128]{2,1,0:T(8,128)(2,1)S(1)}, f32[3,8,128]{2,1,0:T(8,128)S(1)}, f32[8,256]{1,0:T(8,128)S(1)}, f32[8,256]{1,0:T(8,128)S(1)}) custom-call(s32[6]{0:T(128)S(1)} %copy-done.8, bf16[256,6144]{1,0:T(8,128)(2,1)S(1)} %bitcast.9, bf16[256,6144]{1,0:T(8,128)(2,1)S(1)} %bitcast.11, ...), custom_call_target="tpu_custom_call" | custom-call | flops 4000000000 | tf_op jit(solution)/shard_map/prior_weights/pallas_call | solution.py:452
  25.1 4.1 %collective-permute-start.2 = (f32[8,256]{1,0:T(8,128)S(1)}, f32[8,256]{1,0:T(8,128)S(1)}, u32[]{:S(2)}, u32[]{:S(2)}) collective-permute-start(f32[8,256]{1,0:T(8,128)S(1)} %get-tuple-element.45), channel_id=1, source_target_pairs={{32,0},{64,32},{96,64},{128,96},{160,128},{192,160},{224,192},{0,2... | collective-permute-start | bytes 24584 | tf_op jit(solution)/shard_map/ppermute | solution.py:411
  29.2 0.0 collective-permute-done.1.vp_ref
  29.2 5.3 %prior_dscore.1 = (f32[3,8,1024]{2,1,0:T(8,128)S(1)}, f32[3,8,128]{2,1,0:T(8,128)S(1)}, f32[8,256]{1,0:T(8,128)S(1)}) custom-call(s32[6]{0:T(128)S(1)} %copy-done.8, bf16[256,6144]{1,0:T(8,128)(2,1)S(1)} %bitcast.12, bf16[256,768]{1,0:T(8,128)(2,1)S(1)} %bitcast.16, bf16[256,768]{1,0:T(8,128)(2,1)S(1)} %bitcast.19, ...), custom_call_target="tpu_custom_call" | custom-call | flops 4000000000 | tf_op jit(solution)/shard_map/prior_dscore/pallas_call | solution.py:468
  34.6 0.0 copy-start.10
  34.6 0.0 copy-start.4
  34.6 0.0 copy-start.5
  34.6 0.0 collective-permute-done.2.dvh_ref
  34.6 1.2 %gradients.1 = (bf16[48,16,128]{2,1,0:T(8,128)(2,1)S(1)}, bf16[48,16,128]{2,1,0:T(8,128)(2,1)S(1)}) custom-call(s32[6]{0:T(128)S(1)} %copy-done.8, bf16[256,8192]{1,0:T(8,128)(2,1)S(1)} %get-tuple-element.31.normed_ref, f32[8,256]{1,0:T(8,128)S(1)} %get-tuple-element.43.dqm_ref, f32[8,256]{1,0:T(8,128)S(1)} %get-tuple-element.44.dvm_ref, ...), custom_call_target="tpu_custom_call" | custom-call | tf_op jit(solution)/shard_map/gradients/pallas_call | solution.py:542
  35.8 2.0 %collective-permute-start.3 = (bf16[48,16,128]{2,1,0:T(8,128)(2,1)S(1)}, bf16[48,16,128]{2,1,0:T(8,128)(2,1)S(1)}, u32[]{:S(2)}, u32[]{:S(2)}) collective-permute-start(bf16[48,16,128]{2,1,0:T(8,128)(2,1)S(1)} %get-tuple-element.51), channel_id=1, source_target_pairs={{0,1},{1,0},{2,3},{3,2},{4,5},{5,4},{6,7},{7,6},{8,9},{9,8},{10,11... | collective-permute-start | bytes 589832 | tf_op jit(solution)/shard_map/ppermute | solution.py:396
  37.8 1.1 %collective-permute-done.3 = bf16[48,16,128]{2,1,0:T(8,128)(2,1)S(1)} collective-permute-done((bf16[48,16,128]{2,1,0:T(8,128)(2,1)S(1)}, bf16[48,16,128]{2,1,0:T(8,128)(2,1)S(1)}, u32[]{:S(2)}, u32[]{:S(2)}) %collective-permute-start.3) | collective-permute-done | bytes 196640 | tf_op jit(solution)/shard_map/ppermute | solution.py:396
  38.9 0.1 add_convert_fusion
  38.9 10.3 %all_to_all.15 = bf16[16,3,16,128]{3,2,1,0:T(8,128)(2,1)S(1)} all-to-all(bf16[16,3,16,128]{3,2,1,0:T(8,128)(2,1)S(1)} %bitcast.23), channel_id=1, replica_groups={{0,2,32,34,64,66,96,98,128,130,160,162,192,194,224,226},{1,3,33,35,65,6..., dimensions={0} | all-to-all | bytes 393216 | tf_op jit(solution)/shard_map/all_to_all | solution.py:392
  49.3 15.7 %all_to_all.16 = bf16[8,3,16,128]{3,2,1,0:T(8,128)(2,1)S(1)} all-to-all(bf16[8,3,16,128]{3,2,1,0:T(8,128)(2,1)S(1)} %broadcast_in_dim.7), channel_id=1, replica_groups={{0,4,8,12,16,20,24,28},{1,5,9,13,17,21,25,29},{2,6,10,14,18,22,26,30},{..., dimensions={0} | all-to-all | bytes 196608 | tf_op jit(solution)/shard_map/all_to_all | solution.py:392
  65.0 10.1 %all_to_all.17 = bf16[16,3,16,128]{3,2,1,0:T(8,128)(2,1)S(1)} all-to-all(bf16[16,3,16,128]{3,2,1,0:T(8,128)(2,1)S(1)} %broadcast_in_dim.8), channel_id=1, replica_groups={{0,2,32,34,64,66,96,98,128,130,160,162,192,194,224,226},{1,3,33,35,65,6..., dimensions={0} | all-to-all | bytes 393216 | tf_op jit(solution)/shard_map/all_to_all | solution.py:392
  75.1 4.3 %collective-permute-start.4 = (bf16[48,16,128]{2,1,0:T(8,128)(2,1)S(1)}, bf16[48,16,128]{2,1,0:T(8,128)(2,1)S(1)}, u32[]{:S(2)}, u32[]{:S(2)}) collective-permute-start(bf16[48,16,128]{2,1,0:T(8,128)(2,1)S(1)} %bitcast.20), channel_id=1, source_target_pairs={{0,1},{1,0},{2,3},{3,2},{4,5},{5,4},{6,7},{7,6},{8,9},{9,8},{10,11... | collective-permute-start | bytes 589832 | tf_op jit(solution)/shard_map/ppermute | solution.py:396
  79.4 0.0 copy-done.10
  79.5 1.0 %collective-permute-done.4.other_ref = bf16[48,16,128]{2,1,0:T(8,128)(2,1)S(1)} collective-permute-done((bf16[48,16,128]{2,1,0:T(8,128)(2,1)S(1)}, bf16[48,16,128]{2,1,0:T(8,128)(2,1)S(1)}, u32[]{:S(2)}, u32[]{:S(2)}) %collective-permute-start.4) | collective-permute-done | bytes 196640 | tf_op jit(solution)/shard_map/ppermute | solution.py:396
  80.5 0.0 copy-done.4
  80.5 0.0 copy-done.5
  80.5 1.3 %clip.1 = (f32[8,8192]{1,0:T(8,128)}, f32[8,6144]{1,0:T(8,128)}, f32[8,8192]{1,0:T(8,128)}, f32[8,768]{1,0:T(8,128)}, f32[1,8192]{1,0:T(1,128)}) custom-call(bf16[48,16,128]{2,1,0:T(8,128)(2,1)S(1)} %bitcast.21, bf16[48,16,128]{2,1,0:T(8,128)(2,1)S(1)} %collective-permute-done.4.other_ref, bf16[8,8192]{1,0:T(8,128)(2,1)S(1)} %copy-done.5, ...), custom_call_target="tpu_custom_call" | custom-call | tf_op jit(solution)/shard_map/clip/pallas_call | solution.py:557
  (5 shorter events, 0.1 us)
Async XLA Ops:
  2.4 2.2 %copy-start.9 = (bf16[1,256,8192]{2,1,0:T(8,128)(2,1)S(1)}, bf16[1,256,8192]{2,1,0:T(8,128)(2,1)}, u32[]{:S(2)}) copy-start(bf16[1,256,8192]{2,1,0:T(8,128)(2,1)} %param.11) | copy-start | bytes 12582916
  4.6 2.8 %copy-start.2 = (bf16[1,256,768]{2,1,0:T(8,128)(2,1)S(1)}, bf16[1,256,768]{2,1,0:T(8,128)(2,1)}, u32[]{:S(2)}) copy-start(bf16[1,256,768]{2,1,0:T(8,128)(2,1)} %param.13) | copy-start | bytes 1179652
  4.6 2.8 %copy-start.3 = (bf16[1,256,768]{2,1,0:T(8,128)(2,1)S(1)}, bf16[1,256,768]{2,1,0:T(8,128)(2,1)}, u32[]{:S(2)}) copy-start(bf16[1,256,768]{2,1,0:T(8,128)(2,1)} %param.14) | copy-start | bytes 1179652
  4.6 2.8 %copy-start.7 = (bf16[8,768]{1,0:T(8,128)(2,1)S(1)}, bf16[8,768]{1,0:T(8,128)(2,1)}, u32[]{:S(2)}) copy-start(bf16[8,768]{1,0:T(8,128)(2,1)} %vup_ref.7) | copy-start | bytes 36868
  4.6 2.8 %copy-start.8 = (s32[6]{0:T(128)S(1)}, s32[6]{0:T(128)}, u32[]{:S(2)}) copy-start(s32[6]{0:T(128)} %ids_ref.9) | copy-start | bytes 76
  4.6 8.5 %copy-start = (bf16[1,256,6144]{2,1,0:T(8,128)(2,1)S(1)}, bf16[1,256,6144]{2,1,0:T(8,128)(2,1)}, u32[]{:S(2)}) copy-start(bf16[1,256,6144]{2,1,0:T(8,128)(2,1)} %param.12) | copy-start | bytes 9437188
  4.6 8.4 %copy-start.1 = (bf16[1,256,6144]{2,1,0:T(8,128)(2,1)S(1)}, bf16[1,256,6144]{2,1,0:T(8,128)(2,1)}, u32[]{:S(2)}) copy-start(bf16[1,256,6144]{2,1,0:T(8,128)(2,1)} %param.15) | copy-start | bytes 9437188
  4.6 8.4 %copy-start.6 = (bf16[8,6144]{1,0:T(8,128)(2,1)S(1)}, bf16[8,6144]{1,0:T(8,128)(2,1)}, u32[]{:S(2)}) copy-start(bf16[8,6144]{1,0:T(8,128)(2,1)} %qup_ref.5) | copy-start | bytes 294916
  8.1 10.6 %collective-permute-start = (bf16[3,256,128]{2,1,0:T(8,128)(2,1)S(1)}, bf16[3,256,128]{2,1,0:T(8,128)(2,1)S(1)}, u32[]{:S(2)}, u32[]{:S(2)}) collective-permute-start(bf16[3,256,128]{2,1,0:T(8,128)(2,1)S(1)} %get-tuple-element.35), channel_id=1, source_target_pairs={{224,0},{0,32},{32,64},{64,96},{96,128},{128,160},{160,192},{192,2... | collective-permute-start | bytes 589832 | tf_op jit(solution)/shard_map/ppermute | solution.py:411
  11.8 17.5 %collective-permute-start.1 = (bf16[4,256,128]{2,1,0:T(8,128)(2,1)S(1)}, bf16[4,256,128]{2,1,0:T(8,128)(2,1)S(1)}, u32[]{:S(2)}, u32[]{:S(2)}) collective-permute-start(bf16[4,256,128]{2,1,0:T(8,128)(2,1)S(1)} %get-tuple-element.36), channel_id=1, source_target_pairs={{224,0},{0,32},{32,64},{64,96},{96,128},{128,160},{160,192},{192,2... | collective-permute-start | bytes 786440 | tf_op jit(solution)/shard_map/ppermute | solution.py:411
  25.1 9.4 %collective-permute-start.2 = (f32[8,256]{1,0:T(8,128)S(1)}, f32[8,256]{1,0:T(8,128)S(1)}, u32[]{:S(2)}, u32[]{:S(2)}) collective-permute-start(f32[8,256]{1,0:T(8,128)S(1)} %get-tuple-element.45), channel_id=1, source_target_pairs={{32,0},{64,32},{96,64},{128,96},{160,128},{192,160},{224,192},{0,2... | collective-permute-start | bytes 24584 | tf_op jit(solution)/shard_map/ppermute | solution.py:411
  34.6 44.9 %copy-start.10 = (bf16[8192]{0:T(1024)(128)(2,1)S(1)}, bf16[8192]{0:T(1024)(128)(2,1)}, u32[]{:S(2)}) copy-start(bf16[8192]{0:T(1024)(128)(2,1)} %param.16) | copy-start | bytes 49156
  34.6 46.0 %copy-start.4 = (bf16[8,8192]{1,0:T(8,128)(2,1)S(1)}, bf16[8,8192]{1,0:T(8,128)(2,1)}, u32[]{:S(2)}) copy-start(bf16[8,8192]{1,0:T(8,128)(2,1)} %vd_ref.1) | copy-start | bytes 393220
  34.6 46.0 %copy-start.5 = (bf16[8,8192]{1,0:T(8,128)(2,1)S(1)}, bf16[8,8192]{1,0:T(8,128)(2,1)}, u32[]{:S(2)}) copy-start(bf16[8,8192]{1,0:T(8,128)(2,1)} %qd_ref.1) | copy-start | bytes 393220
  35.8 3.1 %collective-permute-start.3 = (bf16[48,16,128]{2,1,0:T(8,128)(2,1)S(1)}, bf16[48,16,128]{2,1,0:T(8,128)(2,1)S(1)}, u32[]{:S(2)}, u32[]{:S(2)}) collective-permute-start(bf16[48,16,128]{2,1,0:T(8,128)(2,1)S(1)} %get-tuple-element.51), channel_id=1, source_target_pairs={{0,1},{1,0},{2,3},{3,2},{4,5},{5,4},{6,7},{7,6},{8,9},{9,8},{10,11... | collective-permute-start | bytes 589832 | tf_op jit(solution)/shard_map/ppermute | solution.py:396
  75.1 5.4 %collective-permute-start.4 = (bf16[48,16,128]{2,1,0:T(8,128)(2,1)S(1)}, bf16[48,16,128]{2,1,0:T(8,128)(2,1)S(1)}, u32[]{:S(2)}, u32[]{:S(2)}) collective-permute-start(bf16[48,16,128]{2,1,0:T(8,128)(2,1)S(1)} %bitcast.20), channel_id=1, source_target_pairs={{0,1},{1,0},{2,3},{3,2},{4,5},{5,4},{6,7},{7,6},{8,9},{9,8},{10,11... | collective-permute-start | bytes 589832 | tf_op jit(solution)/shard_map/ppermute | solution.py:396

commit v4 on v3

--- a/solution.py
+++ b/solution.py
@@ -59,17 +59,9 @@
     vmt_ref[...] = mid_t[RANK:].astype(BF16)
 
 
-def pick_kernel(ids_ref, k_ref, v_ref, vm_ref, vmt_ref, vup_ref, keys_ref, values_ref):
+def pick_kernel(ids_ref, k_ref, after_ref, keys_ref):
     for i in range(3):
-        small = head_cols(ids_ref, 3 + i, HEAD_SIZE)
-        keys_ref[i] = k_ref[:, small]
-        values_ref[i] = adapted(v_ref[:, small], vm_ref[...], vup_ref[:, small])
-    mid_t = vmt_ref[...].astype(F32)
-    pad = jnp.zeros((RANK, HEAD_SIZE), F32)
-    values_ref[3] = jnp.zeros((TOKENS, HEAD_SIZE), BF16)
-    for j in range(2):
-        block = jnp.concatenate([mid_t[:, j * HEAD_SIZE : (j + 1) * HEAD_SIZE], pad], axis=0)
-        values_ref[3, j * 16 : (j + 1) * 16] = block.astype(BF16)
+        keys_ref[i] = k_ref[:, head_cols(ids_ref, 3 + i, HEAD_SIZE)]
 
 
 def head_at(ids_ref, place):
@@ -117,7 +109,8 @@
 
 
 def adapted(frozen, mid, up):
-    return (frozen.astype(F32) + 2.0 * nn(mid, up)).astype(BF16)
+    doubled = (2.0 * mid.astype(F32)).astype(BF16)
+    return (frozen.astype(F32) + nn(doubled, up)).astype(BF16)
 
 
 def own_scores(keys, queries, c, mask):
@@ -164,7 +157,7 @@
 
 def own_kernel(
     ids_ref, q_ref, g_ref, k_ref, v_ref, qm_ref, vm_ref, qmt_ref, vmt_ref, qup_ref, vup_ref,
-    qb_ref, vb_ref, dqm_ref, dvm_ref, q_scr, dq_scr,
+    qb_ref, vb_ref, dqm_ref, dvm_ref, values_ref, q_scr, dq_scr,
 ):
     mask = causal_mask()
     heads = {}
@@ -176,7 +169,9 @@
             keys = k_ref[:, small]
             vup, qup = vup_ref[:, small], qup_ref[:, head_cols(ids_ref, 3 + i, LANES)]
             q_scr[i] = adapted(q_ref[:, head_cols(ids_ref, 3 + i, LANES)], qm_ref[...], qup)
-            heads[i] = (keys, transposed(keys), adapted(v_ref[:, small], vm_ref[...], vup), qup, vup)
+            values = adapted(v_ref[:, small], vm_ref[...], vup)
+            values_ref[i] = values
+            heads[i] = (keys, transposed(keys), values, qup, vup)
         keys, _, values, _, _ = heads[i]
         grads = stacked_grads(g_ref, ids_ref, 3 + i, c, part)
         return own_scores(keys, stacked(q_scr, i, c, part), c, mask), nt(values[: (c + 1) * HALF], grads), grads
@@ -209,6 +204,12 @@
     pipelined(before, after)
     dqm_ref[...] = totals["dq"]
     dvm_ref[...] = totals["dv"]
+    mid_t = vmt_ref[...].astype(F32)
+    pad = jnp.zeros((RANK, HEAD_SIZE), F32)
+    values_ref[3] = jnp.zeros((TOKENS, HEAD_SIZE), BF16)
+    for j in range(2):
+        block = jnp.concatenate([mid_t[:, j * HEAD_SIZE : (j + 1) * HEAD_SIZE], pad], axis=0)
+        values_ref[3, j * 16 : (j + 1) * 16] = block.astype(BF16)
 
 
 def weights_kernel(
@@ -437,10 +438,10 @@
         own_kernel,
         out_shape=[
             struct((3, RANK, LANES), F32), struct((3, RANK, HEAD_SIZE), F32),
-            struct((RANK, TOKENS), F32), struct((RANK, TOKENS), F32),
+            struct((RANK, TOKENS), F32), struct((RANK, TOKENS), F32), struct((4, TOKENS, HEAD_SIZE), BF16),
         ],
         in_specs=[SMEM] + [VMEM] * 10,
-        out_specs=[VMEM] * 4,
+        out_specs=[VMEM] * 5,
         scratch_shapes=[pltpu.VMEM((3, TOKENS, LANES), BF16), pltpu.VMEM((3, LANES, TOKENS), BF16)],
         compiler_params=params(28),
         cost_estimate=cost(1),
@@ -521,18 +522,18 @@
         name="norm",
     )(x, down)
 
-    keys_out, values_out = pl.pallas_call(
+    keys_out = pl.pallas_call(
         pick_kernel,
-        out_shape=[struct((3, TOKENS, HEAD_SIZE), BF16), struct((4, TOKENS, HEAD_SIZE), BF16)],
-        in_specs=[SMEM] + [VMEM] * 5,
-        out_specs=[VMEM] * 2,
+        out_shape=struct((3, TOKENS, HEAD_SIZE), BF16),
+        in_specs=[SMEM] + [VMEM] * 2,
+        out_specs=VMEM,
         compiler_params=params(8),
         name="pick",
-    )(ids, k, v, vm, vmt, vup)
+    )(ids, k, vmt)
     keys_prior = from_behind(keys_out, 1)
+
+    qb1, vb1, dqm1, dvm1, values_out = own_call(ids, q, g, k, v, qm, vm, qmt, vmt, qup, vup)
     values_prior = from_behind(values_out, 1)
-
-    qb1, vb1, dqm1, dvm1 = own_call(ids, q, g, k, v, qm, vm, qmt, vmt, qup, vup)
     w, dvp, vbp, dvm, handed = weights_call(ids, q, g, k, qm, vmt, qup, vup, keys_prior, dvm1)
     handed = from_behind(handed, -1)
     qb2, vb2, dqm = dscore_call(

time: 82.1 us -> 81.6 us (level)
  no operation moved by 1% of the time
where the time goes in v4:
time: 81.6 us; the launch traced here: 81.3 us
  blocking collectives  36.3 us (44%)
  Pallas kernels  23.1 us (28%)
  starting transfers between devices  14.8 us (18%)
  local copies, waits for them, and re-layouts  3.04 us (4%)
  waiting for transfers between devices  2.12 us (3%)
  other arithmetic  1.12 us (1%)
    all_to_all x3, blocking collectives, exchange(): lax.all_to_all(array, BOTH, 0, 0, tiled=True, axis_index_groups=groups)  36.3 us
    ppermute x3, starting transfers between devices, from_behind(): lax.ppermute(block, 'seq', [((i - distance) % 8, i) for i in range(8)])  8.93 us
    pallas_call x1, Pallas kernels, weights_call(): pl.pallas_call(weights_kernel, out_shape=[struct((3, 7 * HALF, LANES), BF...  6.38 us
    ppermute x2, starting transfers between devices, other_core(): return lax.ppermute(array, 'dp', [(i, i ^ 1) for i in range(32)])  5.9 us
    pallas_call x1, Pallas kernels, own_call(): pl.pallas_call(own_kernel, out_shape=[struct((3, RANK, LANES), F32), stru...  5.75 us
    pallas_call x1, Pallas kernels, dscore_call(): pl.pallas_call(dscore_kernel, out_shape=[struct((3, RANK, LANES), F32), s...  5.34 us
    pallas_call x1, Pallas kernels, shards(): pl.pallas_call(norm_kernel, out_shape=[struct((TOKENS, WIDTH), BF16), str...  2.62 us
    unnamed x22, local copies, waits for them, and re-layouts  2.24 us
  transfers between devices with their start and end apart: 5, of which 2 were waited for; matrix products, arithmetic and copies ran while one was open for 0% of the time, Pallas kernels for 21%

profile of v4, /device:TPU:1, one launch (start us, length us, event | category | flops | bytes accessed | tf_op | source)
XLA Modules:
  0.0 81.3 jit_solution(15309724169377629369)
XLA Ops:
  0.6 0.7 broadcast_in_dim.6
  1.4 1.0 %pad_maximum_fusion.down_ref = bf16[32,8192]{1,0:T(8,128)(2,1)S(1)} fusion(bf16[16,8192]{1,0:T(8,128)(2,1)S(1)} %broadcast_in_dim.6, bf16[8,8192]{1,0:T(8,128)(2,1)} %vd_ref.1, bf16[8,8192]{1,0:T(8,128)(2,1)} %qd_ref.1), kind=kLoop, calls=%fused_computation | loop fusion | flops 1572864 | bytes 1048576 | tf_op jit(solution)/shard_map/concatenate | solution.py:501
  2.4 0.0 copy-start.9
  2.4 2.2 %copy-done.9 = bf16[1,256,8192]{2,1,0:T(8,128)(2,1)S(1)} copy-done((bf16[1,256,8192]{2,1,0:T(8,128)(2,1)S(1)}, bf16[1,256,8192]{2,1,0:T(8,128)(2,1)}, u32[]{:S(2)}) %copy-start.9) | copy-done | bytes 4194328
  4.6 0.0 copy-start.2
  4.6 0.0 copy-start.8
  4.6 0.0 copy-start
  4.6 0.0 copy-start.1
  4.6 0.0 copy-start.5
  4.6 0.0 copy-start.6
  4.6 0.0 copy-start.7
  4.6 2.6 %norm.1 = (bf16[256,8192]{1,0:T(8,128)(2,1)S(1)}, bf16[256,8]{1,0:T(8,128)(2,1)S(1)}, bf16[256,8]{1,0:T(8,128)(2,1)S(1)}, bf16[8,256]{1,0:T(8,128)(2,1)S(1)}, bf16[8,256]{1,0:T(8,128)(2,1)S(1)}) custom-call(bf16[256,8192]{1,0:T(8,128)(2,1)S(1)} %bitcast.21, bf16[32,8192]{1,0:T(8,128)(2,1)S(1)} %pad_maximum_fusion.down_ref), custom_call_target="tpu_custom_call" | custom-call | flops 5000000000 | tf_op jit(solution)/shard_map/norm/pallas_call | solution.py:505
  7.2 0.0 copy-done.2
  7.3 0.0 copy-done.8
  7.3 0.6 pick.1
  7.9 3.7 %collective-permute-start = (bf16[3,256,128]{2,1,0:T(8,128)(2,1)S(1)}, bf16[3,256,128]{2,1,0:T(8,128)(2,1)S(1)}, u32[]{:S(2)}, u32[]{:S(2)}) collective-permute-start(bf16[3,256,128]{2,1,0:T(8,128)(2,1)S(1)} %pick.1), channel_id=1, source_target_pairs={{224,0},{0,32},{32,64},{64,96},{96,128},{128,160},{160,192},{192,2... | collective-permute-start | bytes 589832 | tf_op jit(solution)/shard_map/ppermute | solution.py:412
  11.5 0.0 copy-done
  11.5 0.0 copy-done.1
  11.5 0.0 copy-done.5
  11.5 0.0 copy-done.6
  11.5 0.0 copy-done.7
  11.5 5.7 %own_attention.1 = (f32[3,8,1024]{2,1,0:T(8,128)S(1)}, f32[3,8,128]{2,1,0:T(8,128)S(1)}, f32[8,256]{1,0:T(8,128)S(1)}, f32[8,256]{1,0:T(8,128)S(1)}, bf16[4,256,128]{2,1,0:T(8,128)(2,1)S(1)}) custom-call(s32[6]{0:T(128)S(1)} %copy-done.8, bf16[256,6144]{1,0:T(8,128)(2,1)S(1)} %bitcast.8, bf16[256,6144]{1,0:T(8,128)(2,1)S(1)} %bitcast.10, ...), custom_call_target="tpu_custom_call" | custom-call | flops 1000000000 | tf_op jit(solution)/shard_map/own_attention/pallas_call | solution.py:437
  17.3 1.4 %collective-permute-start.1 = (bf16[4,256,128]{2,1,0:T(8,128)(2,1)S(1)}, bf16[4,256,128]{2,1,0:T(8,128)(2,1)S(1)}, u32[]{:S(2)}, u32[]{:S(2)}) collective-permute-start(bf16[4,256,128]{2,1,0:T(8,128)(2,1)S(1)} %get-tuple-element.35), channel_id=1, source_target_pairs={{224,0},{0,32},{32,64},{64,96},{96,128},{128,160},{160,192},{192,2... | collective-permute-start | bytes 786440 | tf_op jit(solution)/shard_map/ppermute | solution.py:412
  18.7 0.0 collective-permute-done.kp_ref
  18.7 6.4 %prior_weights.1 = (bf16[3,896,1024]{2,1,0:T(8,128)(2,1)S(1)}, bf16[3,256,128]{2,1,0:T(8,128)(2,1)S(1)}, f32[3,8,128]{2,1,0:T(8,128)S(1)}, f32[8,256]{1,0:T(8,128)S(1)}, f32[8,256]{1,0:T(8,128)S(1)}) custom-call(s32[6]{0:T(128)S(1)} %copy-done.8, bf16[256,6144]{1,0:T(8,128)(2,1)S(1)} %bitcast.9, bf16[256,6144]{1,0:T(8,128)(2,1)S(1)} %bitcast.11, ...), custom_call_target="tpu_custom_call" | custom-call | flops 4000000000 | tf_op jit(solution)/shard_map/prior_weights/pallas_call | solution.py:453
  25.1 3.9 %collective-permute-start.2 = (f32[8,256]{1,0:T(8,128)S(1)}, f32[8,256]{1,0:T(8,128)S(1)}, u32[]{:S(2)}, u32[]{:S(2)}) collective-permute-start(f32[8,256]{1,0:T(8,128)S(1)} %get-tuple-element.43), channel_id=1, source_target_pairs={{32,0},{64,32},{96,64},{128,96},{160,128},{192,160},{224,192},{0,2... | collective-permute-start | bytes 24584 | tf_op jit(solution)/shard_map/ppermute | solution.py:412
  29.0 0.0 collective-permute-done.1.vp_ref
  29.0 5.3 %prior_dscore.1 = (f32[3,8,1024]{2,1,0:T(8,128)S(1)}, f32[3,8,128]{2,1,0:T(8,128)S(1)}, f32[8,256]{1,0:T(8,128)S(1)}) custom-call(s32[6]{0:T(128)S(1)} %copy-done.8, bf16[256,6144]{1,0:T(8,128)(2,1)S(1)} %bitcast.12, bf16[256,768]{1,0:T(8,128)(2,1)S(1)} %bitcast.16, bf16[256,768]{1,0:T(8,128)(2,1)S(1)} %bitcast.20, ...), custom_call_target="tpu_custom_call" | custom-call | flops 4000000000 | tf_op jit(solution)/shard_map/prior_dscore/pallas_call | solution.py:469
  34.3 0.0 copy-start.10
  34.3 0.0 copy-start.3
  34.3 0.0 copy-start.4
  34.3 0.0 collective-permute-done.2.dvh_ref
  34.3 1.2 %gradients.1 = (bf16[48,16,128]{2,1,0:T(8,128)(2,1)S(1)}, bf16[48,16,128]{2,1,0:T(8,128)(2,1)S(1)}) custom-call(s32[6]{0:T(128)S(1)} %copy-done.8, bf16[256,8192]{1,0:T(8,128)(2,1)S(1)} %get-tuple-element.30.normed_ref, f32[8,256]{1,0:T(8,128)S(1)} %get-tuple-element.41.dqm_ref, f32[8,256]{1,0:T(8,128)S(1)} %get-tuple-element.42.dvm_ref, ...), custom_call_target="tpu_custom_call" | custom-call | tf_op jit(solution)/shard_map/gradients/pallas_call | solution.py:543
  35.5 1.6 %collective-permute-start.3 = (bf16[48,16,128]{2,1,0:T(8,128)(2,1)S(1)}, bf16[48,16,128]{2,1,0:T(8,128)(2,1)S(1)}, u32[]{:S(2)}, u32[]{:S(2)}) collective-permute-start(bf16[48,16,128]{2,1,0:T(8,128)(2,1)S(1)} %get-tuple-element.49), channel_id=1, source_target_pairs={{0,1},{1,0},{2,3},{3,2},{4,5},{5,4},{6,7},{7,6},{8,9},{9,8},{10,11... | collective-permute-start | bytes 589832 | tf_op jit(solution)/shard_map/ppermute | solution.py:397
  37.1 1.1 %collective-permute-done.3 = bf16[48,16,128]{2,1,0:T(8,128)(2,1)S(1)} collective-permute-done((bf16[48,16,128]{2,1,0:T(8,128)(2,1)S(1)}, bf16[48,16,128]{2,1,0:T(8,128)(2,1)S(1)}, u32[]{:S(2)}, u32[]{:S(2)}) %collective-permute-start.3) | collective-permute-done | bytes 196640 | tf_op jit(solution)/shard_map/ppermute | solution.py:397
  38.2 0.1 add_convert_fusion
  38.3 10.5 %all_to_all.15 = bf16[16,3,16,128]{3,2,1,0:T(8,128)(2,1)S(1)} all-to-all(bf16[16,3,16,128]{3,2,1,0:T(8,128)(2,1)S(1)} %bitcast.22), channel_id=1, replica_groups={{0,2,32,34,64,66,96,98,128,130,160,162,192,194,224,226},{1,3,33,35,65,6..., dimensions={0} | all-to-all | bytes 393216 | tf_op jit(solution)/shard_map/all_to_all | solution.py:393
  48.8 15.7 %all_to_all.16 = bf16[8,3,16,128]{3,2,1,0:T(8,128)(2,1)S(1)} all-to-all(bf16[8,3,16,128]{3,2,1,0:T(8,128)(2,1)S(1)} %broadcast_in_dim.7), channel_id=1, replica_groups={{0,4,8,12,16,20,24,28},{1,5,9,13,17,21,25,29},{2,6,10,14,18,22,26,30},{..., dimensions={0} | all-to-all | bytes 196608 | tf_op jit(solution)/shard_map/all_to_all | solution.py:393
  64.5 10.1 %all_to_all.17 = bf16[16,3,16,128]{3,2,1,0:T(8,128)(2,1)S(1)} all-to-all(bf16[16,3,16,128]{3,2,1,0:T(8,128)(2,1)S(1)} %broadcast_in_dim.8), channel_id=1, replica_groups={{0,2,32,34,64,66,96,98,128,130,160,162,192,194,224,226},{1,3,33,35,65,6..., dimensions={0} | all-to-all | bytes 393216 | tf_op jit(solution)/shard_map/all_to_all | solution.py:393
  74.7 4.3 %collective-permute-start.4 = (bf16[48,16,128]{2,1,0:T(8,128)(2,1)S(1)}, bf16[48,16,128]{2,1,0:T(8,128)(2,1)S(1)}, u32[]{:S(2)}, u32[]{:S(2)}) collective-permute-start(bf16[48,16,128]{2,1,0:T(8,128)(2,1)S(1)} %bitcast.17), channel_id=1, source_target_pairs={{0,1},{1,0},{2,3},{3,2},{4,5},{5,4},{6,7},{7,6},{8,9},{9,8},{10,11... | collective-permute-start | bytes 589832 | tf_op jit(solution)/shard_map/ppermute | solution.py:397
  79.0 0.0 copy-done.10
  79.0 1.0 %collective-permute-done.4.other_ref = bf16[48,16,128]{2,1,0:T(8,128)(2,1)S(1)} collective-permute-done((bf16[48,16,128]{2,1,0:T(8,128)(2,1)S(1)}, bf16[48,16,128]{2,1,0:T(8,128)(2,1)S(1)}, u32[]{:S(2)}, u32[]{:S(2)}) %collective-permute-start.4) | collective-permute-done | bytes 196640 | tf_op jit(solution)/shard_map/ppermute | solution.py:397
  80.1 0.0 copy-done.3
  80.1 0.0 copy-done.4
  80.1 1.3 %clip.1 = (f32[8,8192]{1,0:T(8,128)}, f32[8,6144]{1,0:T(8,128)}, f32[8,8192]{1,0:T(8,128)}, f32[8,768]{1,0:T(8,128)}, f32[1,8192]{1,0:T(1,128)}) custom-call(bf16[48,16,128]{2,1,0:T(8,128)(2,1)S(1)} %bitcast.18, bf16[48,16,128]{2,1,0:T(8,128)(2,1)S(1)} %collective-permute-done.4.other_ref, bf16[8,8192]{1,0:T(8,128)(2,1)S(1)} %copy-done.4, ...), custom_call_target="tpu_custom_call" | custom-call | tf_op jit(solution)/shard_map/clip/pallas_call | solution.py:558
  (5 shorter events, 0.1 us)
Async XLA Ops:
  2.4 2.2 %copy-start.9 = (bf16[1,256,8192]{2,1,0:T(8,128)(2,1)S(1)}, bf16[1,256,8192]{2,1,0:T(8,128)(2,1)}, u32[]{:S(2)}) copy-start(bf16[1,256,8192]{2,1,0:T(8,128)(2,1)} %param.11) | copy-start | bytes 12582916
  4.6 2.7 %copy-start.2 = (bf16[1,256,768]{2,1,0:T(8,128)(2,1)S(1)}, bf16[1,256,768]{2,1,0:T(8,128)(2,1)}, u32[]{:S(2)}) copy-start(bf16[1,256,768]{2,1,0:T(8,128)(2,1)} %param.13) | copy-start | bytes 1179652
  4.6 2.7 %copy-start.8 = (s32[6]{0:T(128)S(1)}, s32[6]{0:T(128)}, u32[]{:S(2)}) copy-start(s32[6]{0:T(128)} %ids_ref.9) | copy-start | bytes 76
  4.6 6.9 %copy-start = (bf16[1,256,6144]{2,1,0:T(8,128)(2,1)S(1)}, bf16[1,256,6144]{2,1,0:T(8,128)(2,1)}, u32[]{:S(2)}) copy-start(bf16[1,256,6144]{2,1,0:T(8,128)(2,1)} %param.12) | copy-start | bytes 9437188
  4.6 6.9 %copy-start.1 = (bf16[1,256,6144]{2,1,0:T(8,128)(2,1)S(1)}, bf16[1,256,6144]{2,1,0:T(8,128)(2,1)}, u32[]{:S(2)}) copy-start(bf16[1,256,6144]{2,1,0:T(8,128)(2,1)} %param.15) | copy-start | bytes 9437188
  4.6 6.9 %copy-start.5 = (bf16[1,256,768]{2,1,0:T(8,128)(2,1)S(1)}, bf16[1,256,768]{2,1,0:T(8,128)(2,1)}, u32[]{:S(2)}) copy-start(bf16[1,256,768]{2,1,0:T(8,128)(2,1)} %param.14) | copy-start | bytes 1179652
  4.6 6.9 %copy-start.6 = (bf16[8,6144]{1,0:T(8,128)(2,1)S(1)}, bf16[8,6144]{1,0:T(8,128)(2,1)}, u32[]{:S(2)}) copy-start(bf16[8,6144]{1,0:T(8,128)(2,1)} %qup_ref.5) | copy-start | bytes 294916
  4.6 6.9 %copy-start.7 = (bf16[8,768]{1,0:T(8,128)(2,1)S(1)}, bf16[8,768]{1,0:T(8,128)(2,1)}, u32[]{:S(2)}) copy-start(bf16[8,768]{1,0:T(8,128)(2,1)} %vup_ref.5) | copy-start | bytes 36868
  7.9 10.8 %collective-permute-start = (bf16[3,256,128]{2,1,0:T(8,128)(2,1)S(1)}, bf16[3,256,128]{2,1,0:T(8,128)(2,1)S(1)}, u32[]{:S(2)}, u32[]{:S(2)}) collective-permute-start(bf16[3,256,128]{2,1,0:T(8,128)(2,1)S(1)} %pick.1), channel_id=1, source_target_pairs={{224,0},{0,32},{32,64},{64,96},{96,128},{128,160},{160,192},{192,2... | collective-permute-start | bytes 589832 | tf_op jit(solution)/shard_map/ppermute | solution.py:412
  17.3 11.7 %collective-permute-start.1 = (bf16[4,256,128]{2,1,0:T(8,128)(2,1)S(1)}, bf16[4,256,128]{2,1,0:T(8,128)(2,1)S(1)}, u32[]{:S(2)}, u32[]{:S(2)}) collective-permute-start(bf16[4,256,128]{2,1,0:T(8,128)(2,1)S(1)} %get-tuple-element.35), channel_id=1, source_target_pairs={{224,0},{0,32},{32,64},{64,96},{96,128},{128,160},{160,192},{192,2... | collective-permute-start | bytes 786440 | tf_op jit(solution)/shard_map/ppermute | solution.py:412
  25.1 9.3 %collective-permute-start.2 = (f32[8,256]{1,0:T(8,128)S(1)}, f32[8,256]{1,0:T(8,128)S(1)}, u32[]{:S(2)}, u32[]{:S(2)}) collective-permute-start(f32[8,256]{1,0:T(8,128)S(1)} %get-tuple-element.43), channel_id=1, source_target_pairs={{32,0},{64,32},{96,64},{128,96},{160,128},{192,160},{224,192},{0,2... | collective-permute-start | bytes 24584 | tf_op jit(solution)/shard_map/ppermute | solution.py:412
  34.3 44.7 %copy-start.10 = (bf16[8192]{0:T(1024)(128)(2,1)S(1)}, bf16[8192]{0:T(1024)(128)(2,1)}, u32[]{:S(2)}) copy-start(bf16[8192]{0:T(1024)(128)(2,1)} %param.16) | copy-start | bytes 49156
  34.3 45.8 %copy-start.3 = (bf16[8,8192]{1,0:T(8,128)(2,1)S(1)}, bf16[8,8192]{1,0:T(8,128)(2,1)}, u32[]{:S(2)}) copy-start(bf16[8,8192]{1,0:T(8,128)(2,1)} %vd_ref.1) | copy-start | bytes 393220
  34.3 45.8 %copy-start.4 = (bf16[8,8192]{1,0:T(8,128)(2,1)S(1)}, bf16[8,8192]{1,0:T(8,128)(2,1)}, u32[]{:S(2)}) copy-start(bf16[8,8192]{1,0:T(8,128)(2,1)} %qd_ref.1) | copy-start | bytes 393220
  35.5 2.7 %collective-permute-start.3 = (bf16[48,16,128]{2,1,0:T(8,128)(2,1)S(1)}, bf16[48,16,128]{2,1,0:T(8,128)(2,1)S(1)}, u32[]{:S(2)}, u32[]{:S(2)}) collective-permute-start(bf16[48,16,128]{2,1,0:T(8,128)(2,1)S(1)} %get-tuple-element.49), channel_id=1, source_target_pairs={{0,1},{1,0},{2,3},{3,2},{4,5},{5,4},{6,7},{7,6},{8,9},{9,8},{10,11... | collective-permute-start | bytes 589832 | tf_op jit(solution)/shard_map/ppermute | solution.py:397
  74.7 5.4 %collective-permute-start.4 = (bf16[48,16,128]{2,1,0:T(8,128)(2,1)S(1)}, bf16[48,16,128]{2,1,0:T(8,128)(2,1)S(1)}, u32[]{:S(2)}, u32[]{:S(2)}) collective-permute-start(bf16[48,16,128]{2,1,0:T(8,128)(2,1)S(1)} %bitcast.17), channel_id=1, source_target_pairs={{0,1},{1,0},{2,3},{3,2},{4,5},{5,4},{6,7},{7,6},{8,9},{9,8},{10,11... | collective-permute-start | bytes 589832 | tf_op jit(solution)/shard_map/ppermute | solution.py:397
